TPU v7x, 1024 devices: a whole 8x8x8 slice. The times are simulated.
1024 devices in a mesh: ex: 64 (over y, x), ey: 16 (over z, core).
Axes of the slice: x: 8, y: 8, z: 8, core: 2. Of those that a mesh axis runs over, the one named last changes fastest.
Arguments:
- dyn_field: float32 [72, 512, 2048], P(None, 'ex', 'ey'), may hold values from -6 to 6
- crm_state: float32 [32768, 58, 128], P(('ex', 'ey')), may hold values from -6 to 6
- subcycles: int32 [32768], P(('ex', 'ey')), may hold values from 1 to 12, as said below
- dest_slot: int32 [32768], P(('ex', 'ey')), may hold values from -1 to 31, as said below
Outputs:
- dyn_out: float32 [72, 512, 2048], P(None, 'ex', 'ey')
- crm_out: float32 [32768, 58, 128], P(('ex', 'ey'))
Inputs may be any that keep to these rules, and one draw needn't show every extreme that they name: `subcycles`: some block of each draw has 12 substeps. Within each ey row the subset's blocks, in order of device and block index, are dealt to the row's owners in turn: the r-th goes to owner r modulo the ey axis's length, and dest_slot = owner * 2 + (its index among its device's subset blocks) divided by the ey axis's length, rounded down. Every owner receives exactly 16 blocks, and some device of each row has all 32 of its blocks in the subset.
All inputs are finite; a program needn't handle non-finite values.
Results may differ from a plain program's by a relative error of at most 0.0003.
Values sent between devices are 32-bit elements; how exact they have to be, the bound alone decides.
A program may use at most 32 MiB of HBM per device.

v0:
```python
import jax
import jax.numpy as jnp
from jax import lax
from jax.sharding import PartitionSpec as P

DSTEPS = 3


mixing = 0.2
damping_coefficient = 0.1
phase_change_warming = 0.5
droplet_formation_speed = 0.5
dewpoint_reference_humidity = 0.5
dewpoint_slope = 0.3
spread_rate = 0.2


def with_halo(cells, sides, width):
    for axis, dim in sides:
        count = lax.axis_size(axis)
        head = lax.slice_in_dim(cells, 0, width, axis=dim)
        tail = lax.slice_in_dim(cells, cells.shape[dim] - width, cells.shape[dim], axis=dim)
        cells = jnp.concatenate(
            [
                lax.ppermute(tail, axis, [(i, (i + 1) % count) for i in range(count)]),
                cells,
                lax.ppermute(head, axis, [((i + 1) % count, i) for i in range(count)]),
            ],
            axis=dim,
        )
    return cells


def cloud_update(fields, coarse_cell_sounding, counts, bound):
    tile_clusters = fields.shape[0]
    altitude_layers = fields.shape[1]
    stack_sequence = fields.shape[2] // 2

    def substep(counter, current):
        bisected_pieces = current.reshape(tile_clusters, altitude_layers, 2, stack_sequence)
        across = (
            jnp.roll(bisected_pieces, 1, axis=3)
            + jnp.roll(bisected_pieces, -1, axis=3)
            - 2.0 * bisected_pieces
        )
        padded = jnp.pad(bisected_pieces, ((0, 0), (1, 1), (0, 0), (0, 0)))
        upward = padded[:, 2:] + padded[:, :-2] - 2.0 * bisected_pieces
        turbulent_diffusion_contribution = mixing * (across + upward)
        ambient_warmth = bisected_pieces[:, :, 0]
        specific_humidity = bisected_pieces[:, :, 1]
        excess_humidity = droplet_formation_speed * jnp.maximum(
            specific_humidity
            - dewpoint_reference_humidity * jnp.exp(dewpoint_slope * ambient_warmth),
            0.0,
        )
        pullback_intensity = damping_coefficient * (
            coarse_cell_sounding - jnp.mean(ambient_warmth, axis=-1)
        )
        upcoming_warmth = (
            ambient_warmth
            + turbulent_diffusion_contribution[:, :, 0]
            + pullback_intensity[:, :, None]
            + phase_change_warming * excess_humidity
        )
        upcoming_humidity = (
            specific_humidity + turbulent_diffusion_contribution[:, :, 1] - excess_humidity
        )
        updated_condition = jnp.stack([upcoming_warmth, upcoming_humidity], axis=2).reshape(
            tile_clusters, altitude_layers, 2 * stack_sequence
        )
        return jnp.where((counter < counts)[:, None, None], updated_condition, current)

    finished = lax.fori_loop(0, bound, substep, fields)
    tendency = jnp.mean(finished[:, :, :stack_sequence] - fields[:, :, :stack_sequence], axis=-1)
    return (finished, tendency)


def stencil(padded):
    interior = padded[:, 1:-1, 1:-1]
    near = padded[:, 2:, 1:-1] + padded[:, :-2, 1:-1] + padded[:, 1:-1, 2:] + padded[:, 1:-1, :-2]
    return interior + spread_rate * (near - 4.0 * interior)


def shards(dyn_field, crm_state, subcycles, dest_slot):
    highest = lax.Precision.HIGHEST
    home_blocks = crm_state.shape[0]
    altitude_layers = crm_state.shape[1]
    width = crm_state.shape[2]
    glev = dyn_field.shape[0]
    stride = dyn_field.shape[1] * dyn_field.shape[2] // home_blocks
    coarse_cell_sounding = dyn_field[:altitude_layers].reshape(altitude_layers, -1)[:, ::stride].T
    field = dyn_field
    for repeat in range(DSTEPS):
        field = stencil(with_halo(field, (("ex", 1), ("ey", 2)), 1))
    peers = lax.axis_size("ey")
    capacity = home_blocks // peers
    sending = dest_slot[None, :] == jnp.arange(home_blocks, dtype=jnp.int32)[:, None]
    sending_weights = sending.astype(jnp.float32)
    outgoing = jnp.einsum("sb,blc->slc", sending_weights, crm_state, precision=highest).reshape(
        peers, capacity, altitude_layers, width
    )
    out_host = jnp.einsum(
        "sb,bl->sl", sending_weights, coarse_cell_sounding, precision=highest
    ).reshape(peers, capacity, altitude_layers)
    out_counts = jnp.sum(jnp.where(sending, subcycles[None, :], 0), axis=1).reshape(peers, capacity)
    arrived, arrived_host, arrived_counts = (
        lax.all_to_all(outgoing, "ey", split_axis=0, concat_axis=0, tiled=True),
        lax.all_to_all(out_host, "ey", split_axis=0, concat_axis=0, tiled=True),
        lax.all_to_all(out_counts, "ey", split_axis=0, concat_axis=0, tiled=True),
    )
    flat_state = arrived.reshape(home_blocks, altitude_layers, width)
    flat_host = arrived_host.reshape(home_blocks, altitude_layers)
    flat_counts = arrived_counts.reshape(home_blocks)
    live = flat_counts > 0
    ordering = jnp.cumsum(live.astype(jnp.int32)) - 1
    owned = home_blocks // 2
    packing = live[None, :] & (ordering[None, :] == jnp.arange(owned, dtype=jnp.int32)[:, None])
    packing_weights = packing.astype(jnp.float32)
    packed = jnp.einsum("os,slc->olc", packing_weights, flat_state, precision=highest)
    packed_host = jnp.einsum("os,sl->ol", packing_weights, flat_host, precision=highest)
    packed_counts = jnp.sum(jnp.where(packing, flat_counts[None, :], 0), axis=1).astype(jnp.int32)
    finished, tendency = cloud_update(packed, packed_host, packed_counts, jnp.max(packed_counts))
    back_state = jnp.einsum("os,olc->slc", packing_weights, finished, precision=highest).reshape(
        peers, capacity, altitude_layers, width
    )
    back_tend = jnp.einsum("os,ol->sl", packing_weights, tendency, precision=highest).reshape(
        peers, capacity, altitude_layers
    )
    returned, returned_tend = (
        lax.all_to_all(back_state, "ey", split_axis=0, concat_axis=0, tiled=True),
        lax.all_to_all(back_tend, "ey", split_axis=0, concat_axis=0, tiled=True),
    )
    home_state = jnp.einsum(
        "sb,slc->blc",
        sending_weights,
        returned.reshape(home_blocks, altitude_layers, width),
        precision=highest,
    )
    home_tend = jnp.einsum(
        "sb,sl->bl",
        sending_weights,
        returned_tend.reshape(home_blocks, altitude_layers),
        precision=highest,
    )
    crm_out = jnp.where((dest_slot >= 0)[:, None, None], home_state, crm_state)
    flat_field = field.reshape(glev, -1)
    flat_field = flat_field.at[:altitude_layers, ::stride].add(home_tend.T)
    dyn_out = flat_field.reshape(field.shape)
    return (dyn_out, crm_out)


def solution(mesh):
    placed = (P(None, "ex", "ey"), P(("ex", "ey"), None, None), P(("ex", "ey")), P(("ex", "ey")))
    return jax.shard_map(
        shards,
        mesh=mesh,
        in_specs=placed,
        out_specs=(P(None, "ex", "ey"), P(("ex", "ey"), None, None)),
        check_vma=False,
    )
```

profile of v0, /device:TPU:1, one launch (start us, length us, event | category | flops | bytes accessed | tf_op | source)
XLA Modules:
  0.0 370.8 jit_solution(12315686723436705042)
XLA Ops:
  2.2 18.2 %all-to-all-start = ((s32[16,1,2]{2,1,0:T(1,128)}), s32[16,1,2]{2,1,0:T(1,128)S(1)}, u32[]{:S(2)}, u32[]{:S(2)}) async-start(s32[16,1,2]{2,1,0:T(1,128)} %bitcast.1), calls=%async_computation | async-start | bytes 16384 | tf_op jit(solution)/shard_map/all_to_all | solution.py:109
  21.7 8.2 %collective-permute-start = (f32[72,1,128]{0,1,2:T(1,128)S(1)}, f32[72,1,128]{0,1,2:T(1,128)S(1)}, u32[]{:S(2)}, u32[]{:S(2)}) collective-permute-start(f32[72,1,128]{0,1,2:T(1,128)S(1)} %get-tuple-element.179), channel_id=1, source_target_pairs={{16,0},{32,16},{48,32},{64,48},{80,64},{96,80},{112,96},{128,112},... | collective-permute-start | bytes 110600 | tf_op jit(solution)/shard_map/ppermute | solution.py:27
  35.4 2.8 collective-permute-done.1
  41.3 6.1 %all-to-all-start.2 = ((f32[16,2,58]{2,1,0:T(2,128)}), f32[16,2,58]{2,1,0:T(2,128)S(1)}, u32[]{:S(2)}, u32[]{:S(2)}) async-start(f32[16,2,58]{2,1,0:T(2,128)} %bitcast.6), calls=%async_computation.2 | async-start | bytes 32768 | tf_op jit(solution)/shard_map/all_to_all | solution.py:108
  49.2 5.6 %all-to-all-done.2 = f32[16,2,58]{2,1,0:T(2,128)S(1)} async-done(((f32[16,2,58]{2,1,0:T(2,128)}), f32[16,2,58]{2,1,0:T(2,128)S(1)}, u32[]{:S(2)}, u32[]{:S(2)}) %all-to-all-start.2) | async-done | bytes 7456 | tf_op jit(solution)/shard_map/all_to_all | solution.py:108
  54.7 3.8 %all-to-all-start.1 = ((f32[16,2,58,128]{3,1,2,0:T(2,128)}), f32[16,2,58,128]{3,1,2,0:T(2,128)S(1)}, u32[]{:S(2)}, u32[]{:S(2)}) async-start(f32[16,2,58,128]{3,1,2,0:T(2,128)} %copy.168), calls=%async_computation.1 | async-start | bytes 1900544 | tf_op jit(solution)/shard_map/all_to_all | solution.py:107
  58.6 3.4 collective-permute-start.4
  64.1 6.4 %collective-permute-done.5 = f32[72,1,128]{0,1,2:T(1,128)S(1)} collective-permute-done((f32[72,1,128]{0,1,2:T(1,128)S(1)}, f32[72,1,128]{0,1,2:T(1,128)S(1)}, u32[]{:S(2)}, u32[]{:S(2)}) %collective-permute-start.5) | collective-permute-done | bytes 36896 | tf_op jit(solution)/shard_map/ppermute | solution.py:25
  73.6 8.2 %collective-permute-done.6 = f32[72,10,1]{0,1,2:T(8,128)S(1)} collective-permute-done((f32[72,10,1]{0,1,2:T(8,128)S(1)}, f32[72,10,1]{0,1,2:T(8,128)S(1)}, u32[]{:S(2)}, u32[]{:S(2)}) %collective-permute-start.6) | collective-permute-done | bytes 2912 | tf_op jit(solution)/shard_map/ppermute | solution.py:27
  82.3 3.4 collective-permute-start.8
  88.4 6.1 %collective-permute-done.9 = f32[72,1,128]{0,1,2:T(1,128)S(1)} collective-permute-done((f32[72,1,128]{0,1,2:T(1,128)S(1)}, f32[72,1,128]{0,1,2:T(1,128)S(1)}, u32[]{:S(2)}, u32[]{:S(2)}) %collective-permute-start.9) | collective-permute-done | bytes 36896 | tf_op jit(solution)/shard_map/ppermute | solution.py:25
  99.9 26.5 %while.13 = (s32[]{:T(128)}, f32[16,58,128]{2,0,1:T(8,128)S(1)}, s32[]{:T(128)}, s32[16]{0:T(128)S(1)}, f32[16,58]{0,1:T(8,128)S(1)}, /*index=5*/s32[]{:T(128)}) while((s32[]{:T(128)}, f32[16,58,128]{2,0,1:T(8,128)S(1)}, s32[]{:T(128)}, s32[16]{0:T(128)S(1)}, f32[16,58]{0,1:T(8,128)S(1)}, /*index=5*/s32[]{:T(128)}) %tuple.73), condition=%wide.region_6.7_spmd, body=%wide.region_4.6_spmd.sunk | while | flops 2021202 | bytes 11659561 | solution.py:73
  127.4 32.7 %all-to-all-start.3 = ((f32[16,2,58]{2,1,0:T(2,128)}), f32[16,2,58]{2,1,0:T(2,128)S(1)}, u32[]{:S(2)}, u32[]{:S(2)}) async-start(f32[16,2,58]{2,1,0:T(2,128)} %bitcast.8), calls=%async_computation.3 | async-start | bytes 32768 | tf_op jit(solution)/shard_map/all_to_all | solution.py:131
  162.0 5.5 %all-to-all-done.3 = f32[16,2,58]{2,1,0:T(2,128)S(1)} async-done(((f32[16,2,58]{2,1,0:T(2,128)}), f32[16,2,58]{2,1,0:T(2,128)S(1)}, u32[]{:S(2)}, u32[]{:S(2)}) %all-to-all-start.3) | async-done | bytes 7456 | tf_op jit(solution)/shard_map/all_to_all | solution.py:131
  167.5 3.8 %all-to-all-start.4 = ((f32[16,2,58,128]{3,1,2,0:T(2,128)}), f32[16,2,58,128]{3,1,2,0:T(2,128)S(1)}, u32[]{:S(2)}, u32[]{:S(2)}) async-start(f32[16,2,58,128]{3,1,2,0:T(2,128)} %copy.173), calls=%async_computation.4 | async-start | bytes 1900544 | tf_op jit(solution)/shard_map/all_to_all | solution.py:130
  172.2 195.6 %while.14 = (s32[]{:T(128)}, f32[72,1024]{0,1:T(8,128)S(1)}, s32[32,2]{0,1:T(2,128)S(1)}, f32[32,58]{1,0:T(8,128)S(1)}, s32[]{:T(128)}, /*index=5*/s32[2]{0:T(128)S(1)}) while((s32[]{:T(128)}, f32[72,1024]{0,1:T(8,128)S(1)}, s32[32,2]{0,1:T(2,128)S(1)}, f32[32,58]{1,0:T(8,128)S(1)}, s32[]{:T(128)}, /*index=5*/s32[2]{0:T(128)S(1)}) %tuple.80), condition=%wide.while_cond, body=%wide.while_body.sunk | while | flops 127 | bytes 1299 | solution.py:147
  172.8 2.0 and_reduce_fusion.2
  174.8 2.0 broadcast_select_fusion.5
  179.0 2.0 and_reduce_fusion.2
  181.0 2.0 broadcast_select_fusion.5
  185.1 2.0 and_reduce_fusion.2
  187.1 2.0 broadcast_select_fusion.5
  191.2 2.0 and_reduce_fusion.2
  193.2 2.0 broadcast_select_fusion.5
  197.3 2.0 and_reduce_fusion.2
  199.3 2.0 broadcast_select_fusion.5
  203.4 2.0 and_reduce_fusion.2
  205.4 2.0 broadcast_select_fusion.5
  209.5 2.0 and_reduce_fusion.2
  211.5 2.0 broadcast_select_fusion.5
  215.6 2.0 and_reduce_fusion.2
  217.6 2.0 broadcast_select_fusion.5
  221.8 2.0 and_reduce_fusion.2
  223.8 2.0 broadcast_select_fusion.5
  227.9 2.0 and_reduce_fusion.2
  229.9 2.0 broadcast_select_fusion.5
  234.0 2.0 and_reduce_fusion.2
  236.0 2.0 broadcast_select_fusion.5
  240.1 2.0 and_reduce_fusion.2
  242.1 2.0 broadcast_select_fusion.5
  246.2 2.0 and_reduce_fusion.2
  248.2 2.0 broadcast_select_fusion.5
  252.3 2.0 and_reduce_fusion.2
  254.3 2.0 broadcast_select_fusion.5
  258.4 2.0 and_reduce_fusion.2
  260.4 2.0 broadcast_select_fusion.5
  264.5 2.0 and_reduce_fusion.2
  270.7 2.0 and_reduce_fusion.2
  276.8 2.0 and_reduce_fusion.2
  282.9 2.0 and_reduce_fusion.2
  284.9 2.0 broadcast_select_fusion.5
  289.0 2.0 and_reduce_fusion.2
  295.1 2.0 and_reduce_fusion.2
  301.2 2.0 and_reduce_fusion.2
  307.3 2.0 and_reduce_fusion.2
  313.5 2.0 and_reduce_fusion.2
  319.6 2.0 and_reduce_fusion.2
  325.7 2.0 and_reduce_fusion.2
  331.8 2.0 and_reduce_fusion.2
  337.9 2.0 and_reduce_fusion.2
  344.0 2.0 and_reduce_fusion.2
  350.1 2.0 and_reduce_fusion.2
  356.3 2.0 and_reduce_fusion.2
  362.4 2.0 and_reduce_fusion.2
  (263 shorter events, 154.1 us)
Async XLA Ops:
  0.6 31.2 %copy-start = (f32[32,58,128]{2,0,1:T(8,128)S(1)}, f32[32,58,128]{2,0,1:T(8,128)}, u32[]{:S(2)}) copy-start(f32[32,58,128]{2,0,1:T(8,128)} %param.7) | copy-start | bytes 2850820
  2.2 39.2 %all-to-all-start = ((s32[16,1,2]{2,1,0:T(1,128)}), s32[16,1,2]{2,1,0:T(1,128)S(1)}, u32[]{:S(2)}, u32[]{:S(2)}) async-start(s32[16,1,2]{2,1,0:T(1,128)} %bitcast.1), calls=%async_computation | async-start | bytes 16384 | tf_op jit(solution)/shard_map/all_to_all | solution.py:109
  21.7 13.7 %collective-permute-start = (f32[72,1,128]{0,1,2:T(1,128)S(1)}, f32[72,1,128]{0,1,2:T(1,128)S(1)}, u32[]{:S(2)}, u32[]{:S(2)}) collective-permute-start(f32[72,1,128]{0,1,2:T(1,128)S(1)} %get-tuple-element.179), channel_id=1, source_target_pairs={{16,0},{32,16},{48,32},{64,48},{80,64},{96,80},{112,96},{128,112},... | collective-permute-start | bytes 110600 | tf_op jit(solution)/shard_map/ppermute | solution.py:27
  29.9 1.9 copy-start.3
  29.9 8.3 %collective-permute-start.1 = (f32[72,1,128]{0,1,2:T(1,128)S(1)}, f32[72,1,128]{0,1,2:T(1,128)S(1)}, u32[]{:S(2)}, u32[]{:S(2)}) collective-permute-start(f32[72,1,128]{0,1,2:T(1,128)S(1)} %get-tuple-element.178), channel_id=1, source_target_pairs={{0,16},{16,32},{32,48},{48,64},{64,80},{80,96},{96,112},{112,128},... | collective-permute-start | bytes 110600 | tf_op jit(solution)/shard_map/ppermute | solution.py:25
  31.9 0.9 slice-start
  38.2 10.5 %collective-permute-start.2 = (f32[72,10,1]{0,1,2:T(8,128)S(1)}, f32[72,10,1]{0,1,2:T(8,128)S(1)}, u32[]{:S(2)}, u32[]{:S(2)}) collective-permute-start(f32[72,10,1]{0,1,2:T(8,128)S(1)} %get-tuple-element.172), channel_id=1, source_target_pairs={{1,0},{2,1},{3,2},{4,3},{5,4},{6,5},{7,6},{8,7},{9,8},{10,9},{11,1... | collective-permute-start | bytes 8648 | tf_op jit(solution)/shard_map/ppermute | solution.py:27
  39.8 9.0 %collective-permute-start.3 = (f32[72,10,1]{0,1,2:T(8,128)S(1)}, f32[72,10,1]{0,1,2:T(8,128)S(1)}, u32[]{:S(2)}, u32[]{:S(2)}) collective-permute-start(f32[72,10,1]{0,1,2:T(8,128)S(1)} %get-tuple-element.173), channel_id=1, source_target_pairs={{0,1},{1,2},{2,3},{3,4},{4,5},{5,6},{6,7},{7,8},{8,9},{9,10},{10,1... | collective-permute-start | bytes 8648 | tf_op jit(solution)/shard_map/ppermute | solution.py:25
  41.3 13.4 %all-to-all-start.2 = ((f32[16,2,58]{2,1,0:T(2,128)}), f32[16,2,58]{2,1,0:T(2,128)S(1)}, u32[]{:S(2)}, u32[]{:S(2)}) async-start(f32[16,2,58]{2,1,0:T(2,128)} %bitcast.6), calls=%async_computation.2 | async-start | bytes 32768 | tf_op jit(solution)/shard_map/all_to_all | solution.py:108
  54.7 44.2 %all-to-all-start.1 = ((f32[16,2,58,128]{3,1,2,0:T(2,128)}), f32[16,2,58,128]{3,1,2,0:T(2,128)S(1)}, u32[]{:S(2)}, u32[]{:S(2)}) async-start(f32[16,2,58,128]{3,1,2,0:T(2,128)} %copy.168), calls=%async_computation.1 | async-start | bytes 1900544 | tf_op jit(solution)/shard_map/all_to_all | solution.py:107
  58.6 5.5 %collective-permute-start.4 = (f32[72,1,128]{0,1,2:T(1,128)S(1)}, f32[72,1,128]{0,1,2:T(1,128)S(1)}, u32[]{:S(2)}, u32[]{:S(2)}) collective-permute-start(f32[72,1,128]{0,1,2:T(1,128)S(1)} %get-tuple-element.177), channel_id=1, source_target_pairs={{16,0},{32,16},{48,32},{64,48},{80,64},{96,80},{112,96},{128,112},... | collective-permute-start | bytes 110600 | tf_op jit(solution)/shard_map/ppermute | solution.py:27
  62.1 8.5 %collective-permute-start.5 = (f32[72,1,128]{0,1,2:T(1,128)S(1)}, f32[72,1,128]{0,1,2:T(1,128)S(1)}, u32[]{:S(2)}, u32[]{:S(2)}) collective-permute-start(f32[72,1,128]{0,1,2:T(1,128)S(1)} %get-tuple-element.176), channel_id=1, source_target_pairs={{0,16},{16,32},{32,48},{48,64},{64,80},{80,96},{96,112},{112,128},... | collective-permute-start | bytes 110600 | tf_op jit(solution)/shard_map/ppermute | solution.py:25
  70.6 11.3 %collective-permute-start.6 = (f32[72,10,1]{0,1,2:T(8,128)S(1)}, f32[72,10,1]{0,1,2:T(8,128)S(1)}, u32[]{:S(2)}, u32[]{:S(2)}) collective-permute-start(f32[72,10,1]{0,1,2:T(8,128)S(1)} %get-tuple-element.170), channel_id=1, source_target_pairs={{1,0},{2,1},{3,2},{4,3},{5,4},{6,5},{7,6},{8,7},{9,8},{10,9},{11,1... | collective-permute-start | bytes 8648 | tf_op jit(solution)/shard_map/ppermute | solution.py:27
  72.1 9.7 %collective-permute-start.7 = (f32[72,10,1]{0,1,2:T(8,128)S(1)}, f32[72,10,1]{0,1,2:T(8,128)S(1)}, u32[]{:S(2)}, u32[]{:S(2)}) collective-permute-start(f32[72,10,1]{0,1,2:T(8,128)S(1)} %get-tuple-element.171), channel_id=1, source_target_pairs={{0,1},{1,2},{2,3},{3,4},{4,5},{5,6},{6,7},{7,8},{8,9},{9,10},{10,1... | collective-permute-start | bytes 8648 | tf_op jit(solution)/shard_map/ppermute | solution.py:25
  82.3 6.1 %collective-permute-start.8 = (f32[72,1,128]{0,1,2:T(1,128)S(1)}, f32[72,1,128]{0,1,2:T(1,128)S(1)}, u32[]{:S(2)}, u32[]{:S(2)}) collective-permute-start(f32[72,1,128]{0,1,2:T(1,128)S(1)} %get-tuple-element.175), channel_id=1, source_target_pairs={{16,0},{32,16},{48,32},{64,48},{80,64},{96,80},{112,96},{128,112},... | collective-permute-start | bytes 110600 | tf_op jit(solution)/shard_map/ppermute | solution.py:27
  85.7 8.8 %collective-permute-start.9 = (f32[72,1,128]{0,1,2:T(1,128)S(1)}, f32[72,1,128]{0,1,2:T(1,128)S(1)}, u32[]{:S(2)}, u32[]{:S(2)}) collective-permute-start(f32[72,1,128]{0,1,2:T(1,128)S(1)} %get-tuple-element.174), channel_id=1, source_target_pairs={{0,16},{16,32},{32,48},{48,64},{64,80},{80,96},{96,112},{112,128},... | collective-permute-start | bytes 110600 | tf_op jit(solution)/shard_map/ppermute | solution.py:25
  94.5 3.1 collective-permute-start.10
  95.5 2.1 collective-permute-start.11
  127.4 40.1 %all-to-all-start.3 = ((f32[16,2,58]{2,1,0:T(2,128)}), f32[16,2,58]{2,1,0:T(2,128)S(1)}, u32[]{:S(2)}, u32[]{:S(2)}) async-start(f32[16,2,58]{2,1,0:T(2,128)} %bitcast.8), calls=%async_computation.3 | async-start | bytes 32768 | tf_op jit(solution)/shard_map/all_to_all | solution.py:131
  162.0 9.5 %copy-start.1 = (f32[72,8,128]{0,2,1:T(8,128)S(1)}, f32[72,8,128]{0,2,1:T(8,128)}, u32[]{:S(2)}) copy-start(f32[72,8,128]{0,2,1:T(8,128)} %copy.177) | copy-start | bytes 884740
  167.5 201.2 %all-to-all-start.4 = ((f32[16,2,58,128]{3,1,2,0:T(2,128)}), f32[16,2,58,128]{3,1,2,0:T(2,128)S(1)}, u32[]{:S(2)}, u32[]{:S(2)}) async-start(f32[16,2,58,128]{3,1,2,0:T(2,128)} %copy.173), calls=%async_computation.4 | async-start | bytes 1900544 | tf_op jit(solution)/shard_map/all_to_all | solution.py:130
  171.5 0.7 copy-start.2
where the time goes:
time: 374 us; the launch traced here: 371 us
  other arithmetic  139 us (37%)
  starting transfers between devices  93.3 us (25%)
  local copies, waits for them, and re-layouts  91.1 us (24%)
  waiting for transfers between devices  35.7 us (10%)
  loops' own time  5.9 us (2%)
  matrix products  5.29 us (1%)
    scatter-add x64, other arithmetic  127 us
    scatter-add x96, local copies, waits for them, and re-layouts  67.7 us
    all_to_all x1, starting transfers between devices, shards(): lax.all_to_all(back_tend, 'ey', split_axis=0, concat_axis=0, tiled=True)  32.7 us
    ppermute x6, starting transfers between devices, with_halo(): lax.ppermute(head, axis, [((i + 1) % count, i) for i in range(count)])  19.1 us
    all_to_all x1, starting transfers between devices, shards(): lax.all_to_all(out_counts, 'ey', split_axis=0, concat_axis=0, tiled=True)  18.2 us
    ppermute x6, waiting for transfers between devices, with_halo(): lax.ppermute(tail, axis, [(i, (i + 1) % count) for i in range(count)])  15.3 us
    ppermute x6, starting transfers between devices, with_halo(): lax.ppermute(tail, axis, [(i, (i + 1) % count) for i in range(count)])  9.55 us
    ppermute x6, waiting for transfers between devices, with_halo(): lax.ppermute(head, axis, [((i + 1) % count, i) for i in range(count)])  9.31 us
  transfers between devices with their start and end apart: 17, of which 7 were waited for; matrix products, arithmetic and copies ran while one was open for 56% of the time, Pallas kernels for 0%

commit v1 on v0

v1 whole, which is shorter than its diff:
```python
import functools

import jax
import jax.numpy as jnp
import ml_dtypes
import numpy as np
from jax import lax
from jax.experimental import pallas as pl
from jax.experimental.pallas import tpu as pltpu
from jax.sharding import PartitionSpec as P

F32 = jnp.float32
BF16 = jnp.bfloat16
MESH = pl.DeviceIdType.MESH

GLEV, LEV, COLS, CX, CY, B_DEV, MAXSUB = 72, 58, 64, 8, 128, 32, 12
PAIRS = B_DEV // 2
ROWS = 64
PAD = 8
GROUP = 4
HALO = 3
PACK = 16
PACKS = (GLEV + PACK - 1) // PACK
CHUNKS = 4
RATE = 0.3 * float(np.log2(np.e))
SCALED_T = RATE
SCALED_Q = 2.0


def tables():
    lane = np.arange(128)
    half, col = lane // COLS, lane % COLS
    same = half[:, None] == half[None, :]
    gap = (col[:, None] - col[None, :]) % COLS
    near = same & ((gap == 0) | (gap == 1) | (gap == COLS - 1))
    moist = near.astype(np.float32)
    warm = moist - same.astype(np.float32) / 128.0
    step = np.stack([np.concatenate([m, m]) for m in (warm, moist)])
    pick = np.zeros((128, 256), np.float32)
    pick[32 * (np.arange(256) // COLS), np.arange(256)] = 1.0
    pick = np.concatenate([pick, pick])
    mean = np.zeros((2, 128, 128), np.float32)
    for pair in range(2):
        mean[pair, lane, 32 * (2 * pair + half)] = 1.0 / COLS
    mean = np.concatenate([mean[0], mean[0], mean[1], mean[1]])
    return [t.astype(ml_dtypes.bfloat16) for t in (step, pick, mean)]


def halves(x):
    high = x.astype(BF16)
    low = (x - high.astype(F32)).astype(BF16)
    return jnp.concatenate([high, low], axis=1)


def dot(x, m):
    return jnp.dot(x, m, preferred_element_type=F32)


def kernel(
    sizes, sub_ref, slot_ref, dyn_hbm, crm_hbm, step_ref, pick_ref, mean_ref,
    dyn_out_hbm, crm_out_hbm,
    field, crm, crm_new, temp, moist, first, pull, count,
    tall, send_rows, recv_rows, send_cols, recv_cols, edge, tend, result,
    in_sem, field_sem, out_sem, result_sem, send_sem, recv_sem,
):
    nex, ney = sizes
    ex, ey = lax.axis_index("ex"), lax.axis_index("ey")
    around = [(dx, dy) for dx in (-1, 0, 1) for dy in (-1, 0, 1) if (dx, dy) != (0, 0)]

    def device(dx, dy):
        return (lax.rem(ex + dx + nex, nex), lax.rem(ey + dy + ney, ney))

    barrier = pltpu.get_barrier_semaphore()
    for at in around:
        pl.semaphore_signal(barrier, inc=1, device_id=device(*at), device_id_type=MESH)

    load_field = pltpu.make_async_copy(dyn_hbm, field, field_sem)
    load_field.start()
    per = B_DEV // CHUNKS
    loads = []
    for c in range(CHUNKS):
        part = pl.ds(c * per, per)
        loads.append(pltpu.make_async_copy(crm_hbm.at[part], crm.at[part], in_sem.at[c]))
        loads[-1].start()

    lane8 = lax.broadcasted_iota(jnp.int32, (8, 128), 1)
    left8 = lane8 < COLS
    for p in range(PAIRS):
        both = []
        for b in (2 * p, 2 * p + 1):
            both.append(jnp.where(slot_ref[b] >= 0, sub_ref[b], 0))
        count[p] = jnp.where(left8, both[0], both[1])
    zero = jnp.zeros((8, 128), F32)
    for buf in (temp, moist):
        for side in range(2):
            buf[side, 0:PAD, :] = zero
            buf[side, PAD + PAIRS * ROWS : PAD + PAIRS * ROWS + PAD, :] = zero
            for p in range(PAIRS):
                buf[side, PAD + p * ROWS + ROWS - 8 : PAD + p * ROWS + ROWS, :] = zero

    load_field.wait()
    for r in range(HALO):
        send_rows[0, r] = field[pl.ds(r, GLEV, stride=CX), :]
        send_rows[1, r] = field[pl.ds(CX - HALO + r, GLEV, stride=CX), :]
    for g in range(PACKS):
        head = zero
        tail = zero
        for i in range(min(PACK, GLEV - g * PACK)):
            tile = field[pl.ds((g * PACK + i) * CX, CX), :]
            tile = pltpu.roll(tile, 8 * i, 1) if i else tile
            head = jnp.where(lane8 // 8 == i, tile, head)
            tail = jnp.where(lane8 // 8 == (i - 1) % PACK, tile, tail)
        send_cols[0, g] = head
        send_cols[1, g] = tail

    pl.semaphore_wait(barrier, len(around))
    copies = []
    for k, (dx, dy) in enumerate(around):
        if dy == 0:
            src, dst = send_rows.at[(dx + 1) // 2], recv_rows.at[(1 - dx) // 2]
        else:
            src, dst = send_cols.at[(dy + 1) // 2], recv_cols.at[1 - dx, (1 - dy) // 2]
        copies.append(
            pltpu.make_async_remote_copy(
                src_ref=src,
                dst_ref=dst,
                send_sem=send_sem.at[k],
                recv_sem=recv_sem.at[k],
                device_id=device(dx, dy),
                device_id_type=MESH,
            )
        )
        copies[-1].start()

    for r in range(CX):
        host = field[pl.ds(r, ROWS, stride=CX), :]
        wide = (0.1 * SCALED_T) * dot(halves(host), pick_ref[...])
        for s in range(2):
            pull[pl.ds((2 * r + s) * ROWS, ROWS), :] = wide[:, 128 * s : 128 * s + 128]

    left = lax.broadcasted_iota(jnp.int32, (LEV, 128), 1) < COLS
    for c in range(CHUNKS):
        loads[c].wait()
        for p in range(c * per // 2, (c + 1) * per // 2):
            one, two = crm[2 * p], crm[2 * p + 1]
            t = SCALED_T * jnp.where(left, one, pltpu.roll(two, COLS, 1))
            q = SCALED_Q * jnp.where(left, pltpu.roll(one, COLS, 1), two)
            temp[0, pl.ds(PAD + p * ROWS, LEV), :] = t
            moist[0, pl.ds(PAD + p * ROWS, LEV), :] = q

    real = lax.broadcasted_iota(jnp.int32, (8, 128), 0) < LEV - (ROWS - 8)

    def substep(n, old, new):
        for g in range(PAIRS // GROUP):
            base, rows = PAD + g * GROUP * ROWS, GROUP * ROWS
            here = pl.ds(base, rows)
            t, q = temp[old, here, :], moist[old, here, :]
            mt = dot(halves(t), step_ref[0])
            mq = dot(halves(q), step_ref[1])
            vt = temp[old, pl.ds(base - 1, rows), :] + temp[old, pl.ds(base + 1, rows), :]
            vq = moist[old, pl.ds(base - 1, rows), :] + moist[old, pl.ds(base + 1, rows), :]
            e = jnp.maximum(q - jnp.exp2(t), 0.0)
            t_new = 0.2 * (mt + vt) + (pull[pl.ds(g * rows, rows), :] + (0.125 * SCALED_T) * e)
            q_new = 0.2 * (mq + vq) - 0.5 * e
            masks = []
            for p in range(g * GROUP, (g + 1) * GROUP):
                on = n < count[p]
                masks += [on] * (ROWS // 8 - 1) + [on & real]
            on = jnp.concatenate(masks, axis=0)
            temp[new, here, :] = jnp.where(on, t_new, t)
            moist[new, here, :] = jnp.where(on, q_new, q)

    @pl.loop(0, MAXSUB // 2)
    def _(n):
        substep(2 * n, 0, 1)
        substep(2 * n + 1, 1, 0)

    outs = []
    for c in range(CHUNKS):
        for p in range(c * per // 2, (c + 1) * per // 2):
            t = (1.0 / SCALED_T) * temp[0, pl.ds(PAD + p * ROWS, LEV), :]
            q = (1.0 / SCALED_Q) * moist[0, pl.ds(PAD + p * ROWS, LEV), :]
            crm_new[2 * p] = jnp.where(left, t, pltpu.roll(q, COLS, 1))
            crm_new[2 * p + 1] = jnp.where(left, pltpu.roll(t, COLS, 1), q)
            first[p] = t - jnp.where(left, crm[2 * p], pltpu.roll(crm[2 * p + 1], COLS, 1))
        part = pl.ds(c * per, per)
        outs.append(pltpu.make_async_copy(crm_new.at[part], crm_out_hbm.at[part], out_sem.at[c]))
        outs[-1].start()
    for r in range(CX):
        change = jnp.concatenate([halves(first[2 * r]), halves(first[2 * r + 1])], axis=1)
        tend[pl.ds(r, LEV, stride=CX), :] = dot(change, mean_ref[...])

    for copy in copies:
        copy.wait()
    for r in range(HALO):
        tall[pl.ds(8 - HALO + r, GLEV, stride=24), :] = recv_rows[0, r]
        tall[pl.ds(16 + r, GLEV, stride=24), :] = recv_rows[1, r]
    for level in range(GLEV):
        tall[pl.ds(level * 24 + 8, CX), :] = field[pl.ds(level * CX, CX), :]
    low_lanes = lane8 % 8 < 4
    for g in range(PACKS):
        for at in range(3):
            edge[g, 8 * at : 8 * at + 8, :] = jnp.where(low_lanes, recv_cols[at, 1, g], recv_cols[at, 0, g])

    first_lane, last_lane = lane8 == 0, lane8 == 127

    def spread(c, e):
        cr, cl = pltpu.roll(c, 1, 1), pltpu.roll(c, 127, 1)
        er, el = pltpu.roll(e, 1, 1), pltpu.roll(e, 127, 1)
        c_new = c + (jnp.where(first_lane, er, cr) + jnp.where(last_lane, el, cl))
        e_new = e + (jnp.where(first_lane, cr, er) + jnp.where(last_lane, cl, el))
        return c_new, e_new

    def sums(rows):
        at = [rows(k) for k in range(-HALO, HALO + 1)]
        return at[3], at[2] + at[4], at[1] + at[5], at[0] + at[6]

    for g in range(PACKS):
        packed = sums(lambda k: edge[g, pl.ds(8 + k, 8), :])
        for i in range(min(PACK, GLEV - g * PACK)):
            level = g * PACK + i
            own = pl.ds(level * CX, CX)
            e = [pltpu.roll(x, 128 - 8 * i, 1) if i else x for x in packed]
            c = sums(lambda k: tall[pl.ds(level * 24 + 8 + k, 8), :])
            x, y = spread(c[0], e[0])
            x, y = spread(x + 3.0 * c[1], y + 3.0 * e[1])
            x, y = spread(x + (6.0 * c[0] + 3.0 * c[2]), y + (6.0 * e[0] + 3.0 * e[2]))
            done = 0.008 * (x + (3.0 * c[1] + c[3]))
            result[own, :] = done + tend[own, :] if level < LEV else done
    store = pltpu.make_async_copy(result, dyn_out_hbm, result_sem)
    store.start()
    for out in outs:
        out.wait()
    store.wait()


def shards(sizes, dyn_field, crm_state, subcycles, dest_slot):
    any_space = pl.BlockSpec(memory_space=pl.ANY)
    smem = pl.BlockSpec(memory_space=pltpu.SMEM)
    vmem = pl.BlockSpec(memory_space=pltpu.VMEM)
    state = (2, 2 * PAD + PAIRS * ROWS, 128)
    dyn_out, crm_out = pl.pallas_call(
        functools.partial(kernel, sizes),
        out_shape=(
            jax.ShapeDtypeStruct((GLEV * CX, CY), F32),
            jax.ShapeDtypeStruct(crm_state.shape, F32),
        ),
        in_specs=[smem, smem, any_space, any_space, vmem, vmem, vmem],
        out_specs=(any_space, any_space),
        scratch_shapes=[
            pltpu.VMEM((GLEV * CX, CY), F32),
            pltpu.VMEM((B_DEV, LEV, 128), F32),
            pltpu.VMEM((B_DEV, LEV, 128), F32),
            pltpu.VMEM(state, F32),
            pltpu.VMEM(state, F32),
            pltpu.VMEM((PAIRS, LEV, 128), F32),
            pltpu.VMEM((PAIRS * ROWS, 128), F32),
            pltpu.VMEM((PAIRS, 8, 128), jnp.int32),
            pltpu.VMEM((GLEV * 24, CY), F32),
            pltpu.VMEM((2, HALO, GLEV, CY), F32),
            pltpu.VMEM((2, HALO, GLEV, CY), F32),
            pltpu.VMEM((2, PACKS, 8, 128), F32),
            pltpu.VMEM((3, 2, PACKS, 8, 128), F32),
            pltpu.VMEM((PACKS, 24, 128), F32),
            pltpu.VMEM((GLEV * CX, CY), F32),
            pltpu.VMEM((GLEV * CX, CY), F32),
            pltpu.SemaphoreType.DMA((CHUNKS,)),
            pltpu.SemaphoreType.DMA,
            pltpu.SemaphoreType.DMA((CHUNKS,)),
            pltpu.SemaphoreType.DMA,
            pltpu.SemaphoreType.DMA((8,)),
            pltpu.SemaphoreType.DMA((8,)),
        ],
        compiler_params=pltpu.CompilerParams(
            collective_id=0, has_side_effects=True, vmem_limit_bytes=48 * 1024 * 1024
        ),
    )(
        subcycles, dest_slot, dyn_field.reshape(GLEV * CX, CY), crm_state,
        *[jnp.asarray(t) for t in tables()],
    )
    return dyn_out.reshape(dyn_field.shape), crm_out


def solution(mesh):
    placed = (P(None, "ex", "ey"), P(("ex", "ey"), None, None), P(("ex", "ey")), P(("ex", "ey")))
    return jax.shard_map(
        functools.partial(shards, (mesh.shape["ex"], mesh.shape["ey"])),
        mesh=mesh,
        in_specs=placed,
        out_specs=(P(None, "ex", "ey"), P(("ex", "ey"), None, None)),
        check_vma=False,
    )
```

time: 374 us -> 44.3 us (0.12)
  other arithmetic: 139 us -> 0 us
  starting transfers between devices: 93.3 us -> 0 us
  local copies, waits for them, and re-layouts: 91.1 us -> 4.04 us
  Pallas kernels: 0 us -> 39.3 us
  waiting for transfers between devices: 35.7 us -> 0 us
  loops' own time: 5.9 us -> 0 us
  matrix products: 5.29 us -> 0 us
    scatter-add x64 -> x0, other arithmetic: 127 us -> none
    scatter-add x96 -> x0, local copies, waits for them, and re-layouts: 67.7 us -> none
    all_to_all x5 -> x0, starting transfers between devices: 64.7 us -> none  [the longest x1 32.7 us: shards(): lax.all_to_all(back_tend, 'ey', split_axis=0, concat_axis=0, tiled=True)]
    pallas_call x0 -> x1, Pallas kernels: none -> 39.3 us  [shards(): pl.pallas_call(functools.partial(kernel, sizes), out_shape=(jax.ShapeDtyp...]
    ppermute x12 -> x0, starting transfers between devices: 28.6 us -> none  [the longest x6 19.1 us: with_halo(): lax.ppermute(head, axis, [((i + 1) % count, i) for i in range(count)])]
    ppermute x12 -> x0, waiting for transfers between devices: 24.6 us -> none  [the longest x6 15.3 us: with_halo(): lax.ppermute(tail, axis, [(i, (i + 1) % count) for i in range(count)])]
    all_to_all x5 -> x0, waiting for transfers between devices: 11.1 us -> none  [the longest x1 5.57 us: shards(): lax.all_to_all(out_host, 'ey', split_axis=0, concat_axis=0, tiled=True)]
    reshape x22 -> x0, local copies, waits for them, and re-layouts: 10.4 us -> none  [the longest x12 3.69 us: substep(): current.reshape(tile_clusters, altitude_layers, 2, stack_sequence)]
  transfers between devices with their start and end apart: 17 -> 0, of which waited for: 7 -> 0; matrix products, arithmetic and copies ran while one was open for 56% -> 0% of each run, Pallas kernels for 0% -> 0%
where the time goes in v1:
time: 44.3 us; the launch traced here: 44.1 us
  Pallas kernels  39.3 us (89%)
  local copies, waits for them, and re-layouts  4.04 us (9%)
  between operations  0.74 us (2%)
    pallas_call x1, Pallas kernels, shards(): pl.pallas_call(functools.partial(kernel, sizes), out_shape=(jax.ShapeDtyp...  39.3 us
    unnamed x15, local copies, waits for them, and re-layouts  4.04 us

profile of v1, /device:TPU:1, one launch (start us, length us, event | category | flops | bytes accessed | tf_op | source)
XLA Modules:
  0.0 44.1 jit_solution(3051848240749990750)
XLA Ops:
  0.6 0.0 copy-start
  0.6 0.0 copy-start.1
  0.7 0.0 copy-start.2
  0.7 0.0 copy-start.3
  0.7 0.0 copy-start.4
  0.7 0.0 copy-start.5
  0.7 1.8 %copy.9.crm_hbm = f32[32,58,128]{2,1,0:T(8,128)S(1)} copy(f32[32,58,128]{2,0,1:T(8,128)} %param.8) | data formatting | bytes 1900544 | tf_op args[1]
  2.5 0.0 copy-done
  2.5 0.0 copy-done.1
  2.5 0.0 copy-done.2
  2.5 0.0 copy-done.3
  2.5 0.0 copy-done.4
  2.6 0.0 copy-done.5
  2.6 39.3 %shard_map.86 = (f32[576,128]{1,0:T(8,128)S(1)}, f32[32,58,128]{2,1,0:T(8,128)S(1)}) custom-call(s32[32]{0:T(128)S(1)} %copy-done.4, s32[32]{0:T(128)S(1)} %copy-done.5, f32[576,128]{1,0:T(8,128)S(1)} %bitcast.3, f32[32,58,128]{2,1,0:T(8,128)S(1)} %copy.9.crm_hbm, bf16[2,256,128]{2,1,0:T(8,128)(2,1)S(1)} %copy-done.3, bf16[256,256]{1,0:T(8,128)(2,1)S(1)} %copy-done.2, ...), custom_call_target="tpu_custom_call" | custom-call | tf_op jit(solution)/shard_map/pallas_call | solution.py:242
  41.9 1.5 %copy.10 = f32[32,58,128]{2,0,1:T(8,128)} copy(f32[32,58,128]{2,1,0:T(8,128)S(1)} %get-tuple-element.7) | data formatting | bytes 1900544
  43.4 0.7 %copy.12 = f32[72,8,128]{2,1,0:T(8,128)} copy(f32[72,8,128]{2,1,0:T(8,128)S(1)} %bitcast.2) | data formatting | bytes 589824
Async XLA Ops:
  0.6 1.9 %copy-start = (f32[72,8,128]{2,1,0:T(8,128)S(1)}, f32[72,8,128]{2,1,0:T(8,128)}, u32[]{:S(2)}) copy-start(f32[72,8,128]{2,1,0:T(8,128)} %param.7) | copy-start | bytes 884740
  0.6 1.9 %copy-start.1 = (bf16[512,128]{1,0:T(8,128)(2,1)S(1)}, bf16[512,128]{1,0:T(8,128)(2,1)}, u32[]{:S(2)}) copy-start(bf16[512,128]{1,0:T(8,128)(2,1)} %constant.8.clone.mean_ref) | copy-start | bytes 393220
  0.7 1.9 %copy-start.2 = (bf16[256,256]{1,0:T(8,128)(2,1)S(1)}, bf16[256,256]{1,0:T(8,128)(2,1)}, u32[]{:S(2)}) copy-start(bf16[256,256]{1,0:T(8,128)(2,1)} %constant.7.clone.pick_ref) | copy-start | bytes 393220
  0.7 1.9 %copy-start.3 = (bf16[2,256,128]{2,1,0:T(8,128)(2,1)S(1)}, bf16[2,256,128]{2,1,0:T(8,128)(2,1)}, u32[]{:S(2)}) copy-start(bf16[2,256,128]{2,1,0:T(8,128)(2,1)} %constant.6.clone.step_ref) | copy-start | bytes 393220
  0.7 1.9 %copy-start.4 = (s32[32]{0:T(128)S(1)}, s32[32]{0:T(128)}, u32[]{:S(2)}) copy-start(s32[32]{0:T(128)} %sub_ref.1) | copy-start | bytes 388
  0.7 1.9 %copy-start.5 = (s32[32]{0:T(128)S(1)}, s32[32]{0:T(128)}, u32[]{:S(2)}) copy-start(s32[32]{0:T(128)} %slot_ref.1) | copy-start | bytes 388

commit v2 on v1

v2 whole, which is shorter than its diff:
```python
import functools

import jax
import jax.numpy as jnp
import numpy as np
from jax import lax
from jax.experimental import pallas as pl
from jax.experimental.pallas import tpu as pltpu
from jax.sharding import PartitionSpec as P

F32 = jnp.float32
BF16 = jnp.bfloat16
MESH = pl.DeviceIdType.MESH

GLEV, LEV, COLS, CX, CY, B_DEV, MAXSUB = 72, 58, 64, 8, 128, 32, 12
PER_ROW = B_DEV // CX
STRIDE = CY // PER_ROW
ROWS = LEV * CX
GROWS = GLEV * CX
PAD = 8
SETS = PER_ROW // 2
CUTS = (0, 16, 30, 44, 58)
HALO = 3
PACK = 16
PACKS = (GLEV + PACK - 1) // PACK
GROUPS = GLEV // 8
CHUNKS = 2
VMEM_BYTES = 60 * 1024 * 1024
RATE = 0.3 * float(np.log2(np.e))
SCALED_T = RATE
SCALED_Q = 2.0
AROUND = [(1, 0), (1, -1), (1, 1), (0, -1), (0, 1), (-1, 0), (-1, -1), (-1, 1)]


def tables(step, pick, mean):
    def iotas(shape):
        return (lax.broadcasted_iota(jnp.int32, shape, d) for d in range(2))

    def where(flag, value):
        return jnp.where(flag, value, 0.0)

    row, col = iotas((256, 256))
    gap = (row - col) & (COLS - 1)
    same = row // COLS == col // COLS
    near = same & ((gap == 0) | (gap == 1) | (gap == COLS - 1))
    block = where(near, 1.0) - where(same & (row < 128), 1.0 / 128.0)
    step[0:256, :] = block.astype(BF16)
    step[256:512, :] = block.astype(BF16)
    block = where((row & 127) == STRIDE * (col // COLS), 1.0)
    pick[...] = block.astype(BF16)
    row, col = iotas((256, 128))
    for j in range(SETS):
        block = where(col == STRIDE * (2 * j + (row & 127) // COLS), 1.0 / COLS)
        mean[256 * j : 256 * j + 256, :] = block.astype(BF16)


def split(x):
    high = x.astype(BF16)
    return high, (x - high.astype(F32)).astype(BF16)


def dot(terms, m):
    return jnp.dot(jnp.concatenate(terms, axis=1), m, preferred_element_type=F32)


def kernel(
    sizes, sub_hbm, slot_hbm, dyn_hbm, crm_hbm,
    dyn_hbm_out, crm_hbm_out,
    result, crm_new, field, crm, sub, slot, step, pick, mean, temp, moist, pull,
    tall, send_rows, recv_rows, send_cols, recv_cols, send_far, recv_far, edge,
    load_sem, in_sem, out_sem, send_sem, recv_sem,
):
    nex, ney = sizes
    ex, ey = lax.axis_index("ex"), lax.axis_index("ey")

    def order(x, y):
        index = x * ney + y
        return jnp.where(index == 0, 6 * nex * ney + 5, 10 * index)

    def device(dx, dy):
        return lax.rem(ex + dx + nex, nex), lax.rem(ey + dy + ney, ney)

    mine = order(ex, ey)
    ahead = [order(*device(*at)) < mine for at in AROUND]
    n_ahead = sum(jnp.where(a, 1, 0) for a in ahead)

    barrier = pltpu.get_barrier_semaphore()
    for at, a in zip(AROUND, ahead):
        @pl.when(jnp.logical_not(a))
        def _():
            pl.semaphore_signal(barrier, inc=1, device_id=device(*at), device_id_type=MESH)

    small = [(dyn_hbm, field), (sub_hbm, sub), (slot_hbm, slot)]
    small = [pltpu.make_async_copy(src, dst, load_sem.at[i]) for i, (src, dst) in enumerate(small)]
    for copy in small:
        copy.start()
    loads = []
    per = LEV * B_DEV // CHUNKS
    for c in range(CHUNKS):
        part = pl.ds(c * per, per)
        loads.append(pltpu.make_async_copy(crm_hbm.at[part], crm.at[part], in_sem.at[c]))
        loads[-1].start()

    lane8 = lax.broadcasted_iota(jnp.int32, (8, 128), 1)
    row8 = lax.broadcasted_iota(jnp.int32, (8, 128), 0)
    left8 = lane8 < COLS
    zero = jnp.zeros((8, 128), F32)

    small[0].wait()
    for r in range(HALO):
        send_rows[1, r] = field[pl.ds(CX - 1 - r, GLEV, stride=CX), :]
    for r in range(HALO):
        send_rows[0, r] = field[pl.ds(r, GLEV, stride=CX), :]

    copies = []
    for k, (dx, dy) in enumerate(AROUND):
        side = (dy + 1) // 2
        if dy == 0:
            src, dst = send_rows.at[(dx + 1) // 2], recv_rows.at[(1 - dx) // 2]
        elif dx == 1:
            src, dst = send_far.at[side], recv_far.at[1 - side]
        else:
            src, dst = send_cols.at[side], recv_cols.at[-dx, 1 - side]
        copies.append(
            pltpu.make_async_remote_copy(
                src_ref=src,
                dst_ref=dst,
                send_sem=send_sem.at[k],
                recv_sem=recv_sem.at[k],
                device_id=device(dx, dy),
                device_id_type=MESH,
            )
        )

    def begin(k, flag):
        @pl.when(flag)
        def _():
            copies[k].start()

    @pl.when(n_ahead > 0)
    def _():
        pl.semaphore_wait(barrier, n_ahead)

    for k, (dx, dy) in enumerate(AROUND):
        if dy == 0:
            begin(k, ahead[k])

    for r in range(2):
        head, tail = zero, zero
        for g in range(GROUPS):
            tile = send_rows[1, r, 8 * g : 8 * g + 8, :]
            tile = pltpu.roll(tile, 8 * g, 1) if g else tile
            head = jnp.where(lane8 // 8 == g, tile, head)
            tail = jnp.where(lane8 // 8 == (g - 1) % 16, tile, tail)
        send_far[0, r] = head
        send_far[1, r] = tail
    for g in range(PACKS):
        head, tail = zero, zero
        for i in range(min(PACK, GLEV - g * PACK)):
            tile = field[pl.ds((g * PACK + i) * CX, CX), :]
            tile = pltpu.roll(tile, 8 * i, 1) if i else tile
            head = jnp.where(lane8 // 8 == i, tile, head)
            tail = jnp.where(lane8 // 8 == (i - 1) % PACK, tile, tail)
        send_cols[0, g] = head
        send_cols[1, g] = tail
    for k, (dx, dy) in enumerate(AROUND):
        if dy != 0:
            begin(k, ahead[k])

    small[1].wait()
    small[2].wait()
    active = jnp.where(slot[...] >= 0, sub[...], 0).astype(F32)
    lane32 = lax.broadcasted_iota(jnp.int32, (CX, B_DEV), 1)
    row32 = lax.broadcasted_iota(jnp.int32, (CX, B_DEV), 0)
    spread_out = jnp.broadcast_to(active, (CX, B_DEV))
    counts = []
    for k in range(PER_ROW):
        own = jnp.where(lane32 == PER_ROW * row32 + k, spread_out, 0.0)
        counts.append(jnp.sum(own, axis=1, keepdims=True))
    counts = [jnp.where(left8, counts[2 * j], counts[2 * j + 1]) for j in range(SETS)]

    for side in range(2):
        for j in range(SETS):
            for buf in (temp, moist):
                buf[side, j, 0:PAD, :] = zero
                buf[side, j, PAD + ROWS : PAD + ROWS + PAD, :] = zero

    tables(step, pick, mean)
    for a, b in zip(CUTS[:-1], CUTS[1:]):
        here = pl.ds(a * CX, (b - a) * CX)
        wide = (0.1 * SCALED_T) * dot(split(field[here, :]), pick[...])
        for j in range(SETS):
            pull[j, here, :] = wide[:, 128 * j : 128 * j + 128]

    def warm_and_moist(j, level):
        one, two = (crm[pl.ds(level * B_DEV + 2 * j + i, CX, stride=PER_ROW), :] for i in range(2))
        t = jnp.where(left8, one, pltpu.roll(two, COLS, 1))
        q = jnp.where(left8, pltpu.roll(one, COLS, 1), two)
        return t, q

    for load in loads:
        load.wait()
    for level in range(LEV):
        for j in range(SETS):
            t, q = warm_and_moist(j, level)
            temp[0, j, pl.ds(PAD + level * CX, CX), :] = SCALED_T * t
            moist[0, j, pl.ds(PAD + level * CX, CX), :] = SCALED_Q * q

    def substep(n, old, new):
        for j in range(SETS):
            on = n < counts[j]
            for a, b in zip(CUTS[:-1], CUTS[1:]):
                base, rows = PAD + a * CX, (b - a) * CX
                here, up, down = (pl.ds(base + s, rows) for s in (0, CX, -CX))
                t, q = temp[old, j, here, :], moist[old, j, here, :]
                (t1, t2), (q1, q2) = split(t), split(q)
                across = dot([t1, q1, t2, q2], step[...])
                vt = temp[old, j, up, :] + temp[old, j, down, :]
                vq = moist[old, j, up, :] + moist[old, j, down, :]
                e = jnp.maximum(q - jnp.exp2(t), 0.0)
                t_new = 0.2 * (across[:, :128] + vt) + (pull[j, pl.ds(a * CX, rows), :] + (0.125 * SCALED_T) * e)
                q_new = 0.2 * (across[:, 128:] + vq) - 0.5 * e
                mask = jnp.concatenate([on] * (b - a), axis=0)
                temp[new, j, here, :] = jnp.where(mask, t_new, t)
                moist[new, j, here, :] = jnp.where(mask, q_new, q)

    @pl.loop(0, MAXSUB // 2)
    def _(n):
        now = (2 * n).astype(F32)
        substep(now, 0, 1)
        substep(now + 1.0, 1, 0)

    outs = []
    for c in range(CHUNKS):
        for level in range(c * LEV // CHUNKS, (c + 1) * LEV // CHUNKS):
            for j in range(SETS):
                own = pl.ds(PAD + level * CX, CX)
                t = (1.0 / SCALED_T) * temp[0, j, own, :]
                q = (1.0 / SCALED_Q) * moist[0, j, own, :]
                temp[1, j, own, :] = t - warm_and_moist(j, level)[0]
                at = [pl.ds(level * B_DEV + 2 * j + i, CX, stride=PER_ROW) for i in range(2)]
                crm_new[at[0], :] = jnp.where(left8, t, pltpu.roll(q, COLS, 1))
                crm_new[at[1], :] = jnp.where(left8, pltpu.roll(t, COLS, 1), q)
        part = pl.ds(c * per, per)
        outs.append(pltpu.make_async_copy(crm_new.at[part], crm_hbm_out.at[part], out_sem.at[c]))
        outs[-1].start()

    def answer(dx):
        for k, at in enumerate(AROUND):
            if at[0] == dx:
                pair = AROUND.index((-at[0], -at[1]))
                copies[k].wait_recv()
                begin(pair, jnp.logical_not(ahead[pair]))

    answer(-1)
    answer(0)

    for level in range(GLEV):
        tall[pl.ds(level * 24, 8), :] = zero
        tall[pl.ds(level * 24 + 8, CX), :] = field[pl.ds(level * CX, CX), :]
    for r in range(HALO):
        tall[pl.ds(16 + r, GLEV, stride=24), :] = recv_rows[1, r]
    low_lanes = lane8 % 8 < 4
    for g in range(PACKS):
        edge[g, 0:8, :] = zero
        for at in range(2):
            edge[g, 8 * at + 8 : 8 * at + 16, :] = jnp.where(low_lanes, recv_cols[at, 1, g], recv_cols[at, 0, g])

    first_lane, last_lane = lane8 == 0, lane8 == 127

    def spread(c, e):
        cr, cl = pltpu.roll(c, 1, 1), pltpu.roll(c, 127, 1)
        er, el = pltpu.roll(e, 1, 1), pltpu.roll(e, 127, 1)
        c_new = c + (jnp.where(first_lane, er, cr) + jnp.where(last_lane, el, cl))
        e_new = e + (jnp.where(first_lane, cr, er) + jnp.where(last_lane, cl, el))
        return c_new, e_new

    def sums(rows):
        at = [rows(k) for k in range(-HALO, HALO + 1)]
        return at[3], at[2] + at[4], at[1] + at[5], at[0] + at[6]

    for g in range(PACKS):
        packed = sums(lambda k: edge[g, pl.ds(8 + k, 8), :])
        for i in range(min(PACK, GLEV - g * PACK)):
            level = g * PACK + i
            own = pl.ds(level * CX, CX)
            e = [pltpu.roll(x, 128 - 8 * i, 1) if i else x for x in packed]
            c = sums(lambda k: tall[pl.ds(level * 24 + 8 + k, 8), :])
            x, y = spread(c[0], e[0])
            x, y = spread(x + 3.0 * c[1], y + 3.0 * e[1])
            x, y = spread(x + (6.0 * c[0] + 3.0 * c[2]), y + (6.0 * e[0] + 3.0 * e[2]))
            result[own, :] = 0.008 * (x + (3.0 * c[1] + c[3]))
    for a, b in zip(CUTS[:-1], CUTS[1:]):
        here, padded = pl.ds(a * CX, (b - a) * CX), pl.ds(PAD + a * CX, (b - a) * CX)
        change = [part for j in range(SETS) for part in split(temp[1, j, padded, :])]
        result[here, :] += dot(change, mean[...])

    answer(1)
    far = [jnp.where(low_lanes, recv_far[1, r], recv_far[0, r]) for r in range(2)]
    for g in range(GROUPS):
        e1, e2 = (pltpu.roll(x, 128 - 8 * g, 1) if g else x for x in far)
        h1, h2, h3 = (recv_rows[0, r, 8 * g : 8 * g + 8, :] for r in range(HALO))
        u, v = spread(h1, e1)
        w, _ = spread(u + h2, v + e2)
        for r, add in enumerate((3.0 * (w + h1) + h3, 3.0 * u + h2, h1)):
            at = pl.ds(g * 8 * CX + r, 8, stride=CX)
            result[at, :] += 0.008 * add
    outs.append(pltpu.make_async_copy(result, dyn_hbm_out, out_sem.at[CHUNKS]))
    outs[-1].start()
    for copy in copies:
        copy.wait_send()
    for out in outs:
        out.wait()


def write(result, crm_new, dyn_out, crm_out, sems):
    parts = []
    for src, dst, n in ((crm_new, crm_out, 4), (result, dyn_out, 2)):
        rows = src.shape[0] // n
        for c in range(n):
            part = pl.ds(c * rows, rows)
            parts.append(pltpu.make_async_copy(src.at[part], dst.at[part], sems.at[len(parts)]))
    for part in parts:
        part.start()
    for part in parts:
        part.wait()


def shards(sizes, dyn_field, crm_state, subcycles, dest_slot):
    hbm = pl.BlockSpec(memory_space=pltpu.HBM)
    state = (2, SETS, ROWS + 2 * PAD, 128)
    dyn_shape = jax.ShapeDtypeStruct((GROWS, CY), F32)
    crm_shape = jax.ShapeDtypeStruct((LEV * B_DEV, 128), F32)
    result, crm_new = pl.pallas_call(
        functools.partial(kernel, sizes),
        out_shape=(dyn_shape, crm_shape),
        in_specs=[hbm] * 4,
        out_specs=(hbm, hbm),
        scratch_shapes=[
            pltpu.VMEM((GROWS, CY), F32),
            pltpu.VMEM((LEV * B_DEV, 128), F32),
            pltpu.VMEM((GROWS, CY), F32),
            pltpu.VMEM((LEV * B_DEV, 128), F32),
            pltpu.VMEM((1, B_DEV), jnp.int32),
            pltpu.VMEM((1, B_DEV), jnp.int32),
            pltpu.VMEM((512, 256), BF16),
            pltpu.VMEM((256, 256), BF16),
            pltpu.VMEM((512, 128), BF16),
            pltpu.VMEM(state, F32),
            pltpu.VMEM(state, F32),
            pltpu.VMEM((SETS, ROWS, 128), F32),
            pltpu.VMEM((GLEV * 24, CY), F32),
            pltpu.VMEM((2, HALO, GLEV, CY), F32),
            pltpu.VMEM((2, HALO, GLEV, CY), F32),
            pltpu.VMEM((2, PACKS, 8, 128), F32),
            pltpu.VMEM((2, 2, PACKS, 8, 128), F32),
            pltpu.VMEM((2, 2, 8, 128), F32),
            pltpu.VMEM((2, 2, 8, 128), F32),
            pltpu.VMEM((PACKS, 24, 128), F32),
            pltpu.SemaphoreType.DMA((3,)),
            pltpu.SemaphoreType.DMA((CHUNKS,)),
            pltpu.SemaphoreType.DMA((CHUNKS + 1,)),
            pltpu.SemaphoreType.DMA((8,)),
            pltpu.SemaphoreType.DMA((8,)),
        ],
        compiler_params=pltpu.CompilerParams(
            collective_id=0, has_side_effects=True, vmem_limit_bytes=VMEM_BYTES
        ),
    )(
        subcycles.reshape(1, B_DEV),
        dest_slot.reshape(1, B_DEV),
        dyn_field.reshape(GROWS, CY),
        jnp.transpose(crm_state, (1, 0, 2)).reshape(LEV * B_DEV, 128),
    )
    dyn_out, crm_out = pl.pallas_call(
        write,
        out_shape=(dyn_shape, crm_shape),
        in_specs=[hbm] * 2,
        out_specs=(hbm, hbm),
        scratch_shapes=[pltpu.SemaphoreType.DMA((6,))],
        compiler_params=pltpu.CompilerParams(vmem_limit_bytes=VMEM_BYTES),
    )(result, crm_new)
    crm_out = jnp.transpose(crm_out.reshape(LEV, B_DEV, 128), (1, 0, 2))
    return dyn_out.reshape(dyn_field.shape), crm_out


def solution(mesh):
    placed = (P(None, "ex", "ey"), P(("ex", "ey"), None, None), P(("ex", "ey")), P(("ex", "ey")))
    return jax.shard_map(
        functools.partial(shards, (mesh.shape["ex"], mesh.shape["ey"])),
        mesh=mesh,
        in_specs=placed,
        out_specs=(P(None, "ex", "ey"), P(("ex", "ey"), None, None)),
        check_vma=False,
    )
```

time: 44.3 us -> 107 us (2.42)
  the two profiles are of different devices: /device:TPU:1 before, /device:TPU:127 now
where the time goes in v2:
time: 107 us
  Pallas kernels  106 us (99%)
    pallas_call x1, Pallas kernels, shards(): pl.pallas_call(functools.partial(kernel, sizes), out_shape=(dyn_shape, cr...  67.6 us
    pallas_call x1, Pallas kernels, shards(): pl.pallas_call(write, out_shape=(dyn_shape, crm_shape), in_specs=[hbm] *...  38.9 us

profile of v2, /device:TPU:127, one launch (start us, length us, event | category | flops | bytes accessed | tf_op | source)
XLA Modules:
  0.0 107.1 jit_solution(6991330433387522307)
XLA Ops:
  0.6 67.6 %shard_map.59 = (f32[576,128]{1,0:T(8,128)}, f32[1856,128]{1,0:T(8,128)}) custom-call(s32[1,32]{1,0:T(1,128)} %bitcast.12, s32[1,32]{1,0:T(1,128)} %bitcast.13, f32[576,128]{1,0:T(8,128)} %bitcast.11, f32[1856,128]{1,0:T(8,128)} %bitcast.10), custom_call_target="tpu_custom_call" | custom-call | tf_op jit(solution)/shard_map/pallas_call | solution.py:334
  68.2 38.9 %shard_map.60 = (f32[576,128]{1,0:T(8,128)}, f32[1856,128]{1,0:T(8,128)}) custom-call(f32[576,128]{1,0:T(8,128)} %get-tuple-element.6.result, f32[1856,128]{1,0:T(8,128)} %get-tuple-element.7.crm_new), custom_call_target="tpu_custom_call" | custom-call | tf_op jit(solution)/shard_map/pallas_call | solution.py:375

commit v3 on v2

--- a/solution.py
+++ b/solution.py
@@ -22,6 +22,7 @@
 CUTS = (0, 16, 30, 44, 58)
 HALO = 3
 PACK = 16
+BATCH = 8
 PACKS = (GLEV + PACK - 1) // PACK
 GROUPS = GLEV // 8
 CHUNKS = 2
@@ -266,11 +267,11 @@
         for at in range(2):
             edge[g, 8 * at + 8 : 8 * at + 16, :] = jnp.where(low_lanes, recv_cols[at, 1, g], recv_cols[at, 0, g])
 
-    first_lane, last_lane = lane8 == 0, lane8 == 127
-
     def spread(c, e):
-        cr, cl = pltpu.roll(c, 1, 1), pltpu.roll(c, 127, 1)
-        er, el = pltpu.roll(e, 1, 1), pltpu.roll(e, 127, 1)
+        lane = lax.broadcasted_iota(jnp.int32, c.shape, 1)
+        first_lane, last_lane = lane == 0, lane == CY - 1
+        cr, cl = pltpu.roll(c, 1, 1), pltpu.roll(c, CY - 1, 1)
+        er, el = pltpu.roll(e, 1, 1), pltpu.roll(e, CY - 1, 1)
         c_new = c + (jnp.where(first_lane, er, cr) + jnp.where(last_lane, el, cl))
         e_new = e + (jnp.where(first_lane, cr, er) + jnp.where(last_lane, cl, el))
         return c_new, e_new
@@ -279,17 +280,17 @@
         at = [rows(k) for k in range(-HALO, HALO + 1)]
         return at[3], at[2] + at[4], at[1] + at[5], at[0] + at[6]
 
-    for g in range(PACKS):
+    for first in range(0, GLEV, BATCH):
+        g, slots = first // PACK, [i % PACK for i in range(first, first + BATCH)]
         packed = sums(lambda k: edge[g, pl.ds(8 + k, 8), :])
-        for i in range(min(PACK, GLEV - g * PACK)):
-            level = g * PACK + i
-            own = pl.ds(level * CX, CX)
-            e = [pltpu.roll(x, 128 - 8 * i, 1) if i else x for x in packed]
-            c = sums(lambda k: tall[pl.ds(level * 24 + 8 + k, 8), :])
-            x, y = spread(c[0], e[0])
-            x, y = spread(x + 3.0 * c[1], y + 3.0 * e[1])
-            x, y = spread(x + (6.0 * c[0] + 3.0 * c[2]), y + (6.0 * e[0] + 3.0 * e[2]))
-            result[own, :] = 0.008 * (x + (3.0 * c[1] + c[3]))
+        e = [jnp.concatenate([pltpu.roll(x, 128 - 8 * i, 1) if i else x for i in slots]) for x in packed]
+        c = sums(
+            lambda k: jnp.concatenate([tall[pl.ds((first + i) * 24 + 8 + k, 8), :] for i in range(BATCH)])
+        )
+        x, y = spread(c[0], e[0])
+        x, y = spread(x + 3.0 * c[1], y + 3.0 * e[1])
+        x, y = spread(x + (6.0 * c[0] + 3.0 * c[2]), y + (6.0 * e[0] + 3.0 * e[2]))
+        result[pl.ds(first * CX, BATCH * CX), :] = 0.008 * (x + (3.0 * c[1] + c[3]))
     for a, b in zip(CUTS[:-1], CUTS[1:]):
         here, padded = pl.ds(a * CX, (b - a) * CX), pl.ds(PAD + a * CX, (b - a) * CX)
         change = [part for j in range(SETS) for part in split(temp[1, j, padded, :])]
@@ -297,14 +298,12 @@
 
     answer(1)
     far = [jnp.where(low_lanes, recv_far[1, r], recv_far[0, r]) for r in range(2)]
-    for g in range(GROUPS):
-        e1, e2 = (pltpu.roll(x, 128 - 8 * g, 1) if g else x for x in far)
-        h1, h2, h3 = (recv_rows[0, r, 8 * g : 8 * g + 8, :] for r in range(HALO))
-        u, v = spread(h1, e1)
-        w, _ = spread(u + h2, v + e2)
-        for r, add in enumerate((3.0 * (w + h1) + h3, 3.0 * u + h2, h1)):
-            at = pl.ds(g * 8 * CX + r, 8, stride=CX)
-            result[at, :] += 0.008 * add
+    e1, e2 = (jnp.concatenate([pltpu.roll(x, 128 - 8 * g, 1) if g else x for g in range(GROUPS)]) for x in far)
+    h1, h2, h3 = (recv_rows[0, r] for r in range(HALO))
+    u, v = spread(h1, e1)
+    w, _ = spread(u + h2, v + e2)
+    for r, add in enumerate((3.0 * (w + h1) + h3, 3.0 * u + h2, h1)):
+        result[pl.ds(r, GLEV, stride=CX), :] += 0.008 * add
     outs.append(pltpu.make_async_copy(result, dyn_hbm_out, out_sem.at[CHUNKS]))
     outs[-1].start()
     for copy in copies:
@@ -313,17 +312,21 @@
         out.wait()
 
 
-def write(result, crm_new, dyn_out, crm_out, sems):
-    parts = []
-    for src, dst, n in ((crm_new, crm_out, 4), (result, dyn_out, 2)):
+def write(result, crm_new, dyn_out, crm_out, result_held, crm_held, sems):
+    ins, outs = [], []
+    for src, held, dst, n in ((result, result_held, dyn_out, 1), (crm_new, crm_held, crm_out, 4)):
         rows = src.shape[0] // n
         for c in range(n):
             part = pl.ds(c * rows, rows)
-            parts.append(pltpu.make_async_copy(src.at[part], dst.at[part], sems.at[len(parts)]))
-    for part in parts:
-        part.start()
-    for part in parts:
-        part.wait()
+            ins.append(pltpu.make_async_copy(src.at[part], held.at[part], sems.at[0, len(ins)]))
+            outs.append(pltpu.make_async_copy(held.at[part], dst.at[part], sems.at[1, len(outs)]))
+    for load in ins:
+        load.start()
+    for load, store in zip(ins, outs):
+        load.wait()
+        store.start()
+    for store in outs:
+        store.wait()
 
 
 def shards(sizes, dyn_field, crm_state, subcycles, dest_slot):
@@ -377,7 +380,11 @@
         out_shape=(dyn_shape, crm_shape),
         in_specs=[hbm] * 2,
         out_specs=(hbm, hbm),
-        scratch_shapes=[pltpu.SemaphoreType.DMA((6,))],
+        scratch_shapes=[
+            pltpu.VMEM((GROWS, CY), F32),
+            pltpu.VMEM((LEV * B_DEV, 128), F32),
+            pltpu.SemaphoreType.DMA((2, 5)),
+        ],
         compiler_params=pltpu.CompilerParams(vmem_limit_bytes=VMEM_BYTES),
     )(result, crm_new)
     crm_out = jnp.transpose(crm_out.reshape(LEV, B_DEV, 128), (1, 0, 2))

time: 107 us -> 44 us (0.41)
  Pallas kernels: 106 us -> 43.2 us
    pallas_call x1, Pallas kernels: 38.9 us -> 2.08 us  [shards(): pl.pallas_call(write, out_shape=(dyn_shape, crm_shape), in_specs=[hbm] *...]
    pallas_call x1, Pallas kernels: 67.6 us -> 41.1 us  [shards(): pl.pallas_call(functools.partial(kernel, sizes), out_shape=(dyn_shape, cr...]
where the time goes in v3:
time: 44 us; the launch traced here: 43.8 us
  Pallas kernels  43.2 us (98%)
  between operations  0.64 us (1%)
    pallas_call x1, Pallas kernels, shards(): pl.pallas_call(functools.partial(kernel, sizes), out_shape=(dyn_shape, cr...  41.1 us
    pallas_call x1, Pallas kernels, shards(): pl.pallas_call(write, out_shape=(dyn_shape, crm_shape), in_specs=[hbm] *...  2.08 us

profile of v3, /device:TPU:127, one launch (start us, length us, event | category | flops | bytes accessed | tf_op | source)
XLA Modules:
  0.0 43.8 jit_solution(4501723822978468873)
XLA Ops:
  0.6 41.1 %shard_map.59 = (f32[576,128]{1,0:T(8,128)}, f32[1856,128]{1,0:T(8,128)}) custom-call(s32[1,32]{1,0:T(1,128)} %bitcast.12, s32[1,32]{1,0:T(1,128)} %bitcast.13, f32[576,128]{1,0:T(8,128)} %bitcast.11, f32[1856,128]{1,0:T(8,128)} %bitcast.10), custom_call_target="tpu_custom_call" | custom-call | tf_op jit(solution)/shard_map/pallas_call | solution.py:337
  41.8 2.1 %shard_map.60 = (f32[576,128]{1,0:T(8,128)}, f32[1856,128]{1,0:T(8,128)}) custom-call(f32[576,128]{1,0:T(8,128)} %get-tuple-element.6.result, f32[1856,128]{1,0:T(8,128)} %get-tuple-element.7.crm_new), custom_call_target="tpu_custom_call" | custom-call | tf_op jit(solution)/shard_map/pallas_call | solution.py:378

commit v4 on v3

--- a/solution.py
+++ b/solution.py
@@ -74,20 +74,20 @@
     nex, ney = sizes
     ex, ey = lax.axis_index("ex"), lax.axis_index("ey")
 
-    def order(x, y):
-        index = x * ney + y
-        return jnp.where(index == 0, 6 * nex * ney + 5, 10 * index)
-
     def device(dx, dy):
         return lax.rem(ex + dx + nex, nex), lax.rem(ey + dy + ney, ney)
 
-    mine = order(ex, ey)
-    ahead = [order(*device(*at)) < mine for at in AROUND]
-    n_ahead = sum(jnp.where(a, 1, 0) for a in ahead)
+    def answers(dx):
+        return ex == 0 if dx == -1 else ex < 0
+
+    def awaited(dx):
+        return ex == nex - 1 if dx == 1 else ex < 0
+
+    cloud_first = (ex < nex // 4) & (ex + ey > 0)
 
     barrier = pltpu.get_barrier_semaphore()
-    for at, a in zip(AROUND, ahead):
-        @pl.when(jnp.logical_not(a))
+    for at in AROUND:
+        @pl.when(jnp.logical_not(awaited(at[0])))
         def _():
             pl.semaphore_signal(barrier, inc=1, device_id=device(*at), device_id_type=MESH)
 
@@ -118,10 +118,10 @@
         side = (dy + 1) // 2
         if dy == 0:
             src, dst = send_rows.at[(dx + 1) // 2], recv_rows.at[(1 - dx) // 2]
-        elif dx == 1:
-            src, dst = send_far.at[side], recv_far.at[1 - side]
+        elif dx == 0:
+            src, dst = send_cols.at[side], recv_cols.at[1 - side]
         else:
-            src, dst = send_cols.at[side], recv_cols.at[-dx, 1 - side]
+            src, dst = send_far.at[(dx + 1) // 2, side], recv_far.at[(1 - dx) // 2, 1 - side]
         copies.append(
             pltpu.make_async_remote_copy(
                 src_ref=src,
@@ -133,28 +133,16 @@
             )
         )
 
-    def begin(k, flag):
-        @pl.when(flag)
-        def _():
-            copies[k].start()
-
-    @pl.when(n_ahead > 0)
-    def _():
-        pl.semaphore_wait(barrier, n_ahead)
-
-    for k, (dx, dy) in enumerate(AROUND):
-        if dy == 0:
-            begin(k, ahead[k])
-
-    for r in range(2):
-        head, tail = zero, zero
-        for g in range(GROUPS):
-            tile = send_rows[1, r, 8 * g : 8 * g + 8, :]
-            tile = pltpu.roll(tile, 8 * g, 1) if g else tile
-            head = jnp.where(lane8 // 8 == g, tile, head)
-            tail = jnp.where(lane8 // 8 == (g - 1) % 16, tile, tail)
-        send_far[0, r] = head
-        send_far[1, r] = tail
+    for end in range(2):
+        for r in range(2):
+            head, tail = zero, zero
+            for g in range(GROUPS):
+                tile = send_rows[end, r, 8 * g : 8 * g + 8, :]
+                tile = pltpu.roll(tile, 8 * g, 1) if g else tile
+                head = jnp.where(lane8 // 8 == g, tile, head)
+                tail = jnp.where(lane8 // 8 == (g - 1) % 16, tile, tail)
+            send_far[end, 0, r] = head
+            send_far[end, 1, r] = tail
     for g in range(PACKS):
         head, tail = zero, zero
         for i in range(min(PACK, GLEV - g * PACK)):
@@ -164,9 +152,14 @@
             tail = jnp.where(lane8 // 8 == (i - 1) % PACK, tile, tail)
         send_cols[0, g] = head
         send_cols[1, g] = tail
-    for k, (dx, dy) in enumerate(AROUND):
-        if dy != 0:
-            begin(k, ahead[k])
+
+    def exchange():
+        n = len(AROUND) - jnp.where(ex == 0, 3, 0)
+        pl.semaphore_wait(barrier, n)
+        for (dx, dy), copy in zip(AROUND, copies):
+            pl.when(jnp.logical_not(answers(dx)))(copy.start)
+
+    pl.when(jnp.logical_not(cloud_first))(exchange)
 
     small[1].wait()
     small[2].wait()
@@ -246,26 +239,7 @@
         outs.append(pltpu.make_async_copy(crm_new.at[part], crm_hbm_out.at[part], out_sem.at[c]))
         outs[-1].start()
 
-    def answer(dx):
-        for k, at in enumerate(AROUND):
-            if at[0] == dx:
-                pair = AROUND.index((-at[0], -at[1]))
-                copies[k].wait_recv()
-                begin(pair, jnp.logical_not(ahead[pair]))
-
-    answer(-1)
-    answer(0)
-
-    for level in range(GLEV):
-        tall[pl.ds(level * 24, 8), :] = zero
-        tall[pl.ds(level * 24 + 8, CX), :] = field[pl.ds(level * CX, CX), :]
-    for r in range(HALO):
-        tall[pl.ds(16 + r, GLEV, stride=24), :] = recv_rows[1, r]
-    low_lanes = lane8 % 8 < 4
-    for g in range(PACKS):
-        edge[g, 0:8, :] = zero
-        for at in range(2):
-            edge[g, 8 * at + 8 : 8 * at + 16, :] = jnp.where(low_lanes, recv_cols[at, 1, g], recv_cols[at, 0, g])
+    pl.when(cloud_first)(exchange)
 
     def spread(c, e):
         lane = lax.broadcasted_iota(jnp.int32, c.shape, 1)
@@ -276,34 +250,76 @@
         e_new = e + (jnp.where(first_lane, cr, er) + jnp.where(last_lane, cl, el))
         return c_new, e_new
 
-    def sums(rows):
-        at = [rows(k) for k in range(-HALO, HALO + 1)]
-        return at[3], at[2] + at[4], at[1] + at[5], at[0] + at[6]
-
-    for first in range(0, GLEV, BATCH):
-        g, slots = first // PACK, [i % PACK for i in range(first, first + BATCH)]
-        packed = sums(lambda k: edge[g, pl.ds(8 + k, 8), :])
-        e = [jnp.concatenate([pltpu.roll(x, 128 - 8 * i, 1) if i else x for i in slots]) for x in packed]
-        c = sums(
-            lambda k: jnp.concatenate([tall[pl.ds((first + i) * 24 + 8 + k, 8), :] for i in range(BATCH)])
-        )
-        x, y = spread(c[0], e[0])
-        x, y = spread(x + 3.0 * c[1], y + 3.0 * e[1])
-        x, y = spread(x + (6.0 * c[0] + 3.0 * c[2]), y + (6.0 * e[0] + 3.0 * e[2]))
-        result[pl.ds(first * CX, BATCH * CX), :] = 0.008 * (x + (3.0 * c[1] + c[3]))
+    for level in range(GLEV):
+        tall[pl.ds(level * 24, 8), :] = zero
+        tall[pl.ds(level * 24 + 8, CX), :] = field[pl.ds(level * CX, CX), :]
+        tall[pl.ds(level * 24 + 16, 8), :] = zero
+    for start in range(0, GLEV, BATCH):
+        at = [
+            jnp.concatenate([tall[pl.ds((start + i) * 24 + 8 + k, 8), :] for i in range(BATCH)])
+            for k in range(-HALO, HALO + 1)
+        ]
+        c0, c1, c2, c3 = at[3], at[2] + at[4], at[1] + at[5], at[0] + at[6]
+        x, y = spread(c0, jnp.zeros_like(c0))
+        x, y = spread(x + 3.0 * c1, y)
+        x, y = spread(x + (6.0 * c0 + 3.0 * c2), y)
+        result[pl.ds(start * CX, BATCH * CX), :] = 0.008 * (x + (3.0 * c1 + c3))
     for a, b in zip(CUTS[:-1], CUTS[1:]):
         here, padded = pl.ds(a * CX, (b - a) * CX), pl.ds(PAD + a * CX, (b - a) * CX)
         change = [part for j in range(SETS) for part in split(temp[1, j, padded, :])]
         result[here, :] += dot(change, mean[...])
 
-    answer(1)
-    far = [jnp.where(low_lanes, recv_far[1, r], recv_far[0, r]) for r in range(2)]
-    e1, e2 = (jnp.concatenate([pltpu.roll(x, 128 - 8 * g, 1) if g else x for g in range(GROUPS)]) for x in far)
-    h1, h2, h3 = (recv_rows[0, r] for r in range(HALO))
-    u, v = spread(h1, e1)
-    w, _ = spread(u + h2, v + e2)
-    for r, add in enumerate((3.0 * (w + h1) + h3, 3.0 * u + h2, h1)):
-        result[pl.ds(r, GLEV, stride=CX), :] += 0.008 * add
+    def take(dx):
+        for k, at in enumerate(AROUND):
+            if at[0] == dx:
+                copies[k].wait_recv()
+
+    low_lanes = lane8 % 8 < 4
+    for side in range(2):
+        edge[side, 0:8, :] = zero
+        edge[side, 16:24, :] = zero
+
+    take(0)
+    for g in range(PACKS):
+        sides = []
+        for side in range(2):
+            halo = recv_cols[side, g]
+            beyond = (lane8 % 8 >= 5) if side == 0 else (lane8 % 8 < 3)
+            valid = (lane8 % 8 >= 5) | (lane8 % 8 < 3)
+            halo = jnp.where(beyond, halo, 0.0)
+            edge[side, 8:16, :] = halo
+            at = [edge[side, 8 + k : 16 + k, :] for k in range(-HALO, HALO + 1)]
+            c0, c1, c2, c3 = halo, at[2] + at[4], at[1] + at[5], at[0] + at[6]
+
+            def near(x):
+                return x + jnp.where(valid, pltpu.roll(x, 1, 1) + pltpu.roll(x, CY - 1, 1), 0.0)
+
+            x = near(c0)
+            x = near(x + 3.0 * c1)
+            x = near(x + (6.0 * c0 + 3.0 * c2))
+            sides.append(0.008 * x)
+        both = jnp.where(low_lanes, sides[0], sides[1])
+        levels = range(g * PACK, min(GLEV, g * PACK + PACK))
+        add = jnp.concatenate([pltpu.roll(both, (128 - 8 * (i % PACK)) % 128, 1) if i % PACK else both for i in levels])
+        lane = lax.broadcasted_iota(jnp.int32, add.shape, 1)
+        own = pl.ds(levels[0] * CX, len(levels) * CX)
+        result[own, :] += jnp.where((lane < 3) | (lane >= CY - 3), add, 0.0)
+
+    for dx in (-1, 1):
+        take(dx)
+        end = (1 - dx) // 2
+        far = [jnp.where(low_lanes, recv_far[end, 1, r], recv_far[end, 0, r]) for r in range(2)]
+        e1, e2 = (
+            jnp.concatenate([pltpu.roll(x, 128 - 8 * g, 1) if g else x for g in range(GROUPS)]) for x in far
+        )
+        h1, h2, h3 = (recv_rows[end, r] for r in range(HALO))
+        u, v = spread(h1, e1)
+        w, _ = spread(u + h2, v + e2)
+        for r, add in enumerate((3.0 * (w + h1) + h3, 3.0 * u + h2, h1)):
+            result[pl.ds(CX - 1 - r if end else r, GLEV, stride=CX), :] += 0.008 * add
+        for (ax, _), copy in zip(AROUND, copies):
+            if ax == -dx:
+                pl.when(answers(ax))(copy.start)
     outs.append(pltpu.make_async_copy(result, dyn_hbm_out, out_sem.at[CHUNKS]))
     outs[-1].start()
     for copy in copies:
@@ -356,10 +372,10 @@
             pltpu.VMEM((2, HALO, GLEV, CY), F32),
             pltpu.VMEM((2, HALO, GLEV, CY), F32),
             pltpu.VMEM((2, PACKS, 8, 128), F32),
-            pltpu.VMEM((2, 2, PACKS, 8, 128), F32),
-            pltpu.VMEM((2, 2, 8, 128), F32),
-            pltpu.VMEM((2, 2, 8, 128), F32),
-            pltpu.VMEM((PACKS, 24, 128), F32),
+            pltpu.VMEM((2, PACKS, 8, 128), F32),
+            pltpu.VMEM((2, 2, 2, 8, 128), F32),
+            pltpu.VMEM((2, 2, 2, 8, 128), F32),
+            pltpu.VMEM((2, 24, 128), F32),
             pltpu.SemaphoreType.DMA((3,)),
             pltpu.SemaphoreType.DMA((CHUNKS,)),
             pltpu.SemaphoreType.DMA((CHUNKS + 1,)),

time: 44 us -> 35.5 us (0.81)
  the two profiles are of different devices: /device:TPU:127 before, /device:TPU:126 now
where the time goes in v4:
time: 35.5 us; the launch traced here: 35.3 us
  Pallas kernels  34.6 us (97%)
  between operations  0.64 us (2%)
    pallas_call x1, Pallas kernels, shards(): pl.pallas_call(functools.partial(kernel, sizes), out_shape=(dyn_shape, cr...  32.5 us
    pallas_call x1, Pallas kernels, shards(): pl.pallas_call(write, out_shape=(dyn_shape, crm_shape), in_specs=[hbm] *...  2.08 us

profile of v4, /device:TPU:126, one launch (start us, length us, event | category | flops | bytes accessed | tf_op | source)
XLA Modules:
  0.0 35.3 jit_solution(2344695369019686503)
XLA Ops:
  0.6 32.5 %shard_map.59 = (f32[576,128]{1,0:T(8,128)}, f32[1856,128]{1,0:T(8,128)}) custom-call(s32[1,32]{1,0:T(1,128)} %bitcast.12, s32[1,32]{1,0:T(1,128)} %bitcast.13, f32[576,128]{1,0:T(8,128)} %bitcast.11, f32[1856,128]{1,0:T(8,128)} %bitcast.10), custom_call_target="tpu_custom_call" | custom-call | tf_op jit(solution)/shard_map/pallas_call | solution.py:353
  33.2 2.1 %shard_map.60 = (f32[576,128]{1,0:T(8,128)}, f32[1856,128]{1,0:T(8,128)}) custom-call(f32[576,128]{1,0:T(8,128)} %get-tuple-element.6.result, f32[1856,128]{1,0:T(8,128)} %get-tuple-element.7.crm_new), custom_call_target="tpu_custom_call" | custom-call | tf_op jit(solution)/shard_map/pallas_call | solution.py:394

commit v5 on v4

--- a/solution.py
+++ b/solution.py
@@ -30,7 +30,7 @@
 RATE = 0.3 * float(np.log2(np.e))
 SCALED_T = RATE
 SCALED_Q = 2.0
-AROUND = [(1, 0), (1, -1), (1, 1), (0, -1), (0, 1), (-1, 0), (-1, -1), (-1, 1)]
+AROUND = [(0, 1), (1, 1), (-1, 1), (0, -1), (1, -1), (-1, -1), (1, 0), (-1, 0)]
 
 
 def tables(step, pick, mean):
@@ -77,17 +77,20 @@
     def device(dx, dy):
         return lax.rem(ex + dx + nex, nex), lax.rem(ey + dy + ney, ney)
 
-    def answers(dx):
-        return ex == 0 if dx == -1 else ex < 0
-
-    def awaited(dx):
-        return ex == nex - 1 if dx == 1 else ex < 0
-
-    cloud_first = (ex < nex // 4) & (ex + ey > 0)
+    first = (ex == 0) & (ey == 0)
+    last_ey = ey == ney - 1
+
+    def answers(dx, dy):
+        x, y = device(dx, dy)
+        to_first = (x == 0) & (y == 0) & jnp.logical_not(last_ey)
+        return to_first | (ey == 0) if dy == -1 else to_first
+
+    def awaited(dx, dy):
+        return last_ey | first if dy == 1 else first if dy == 0 else first & (ey > 0)
 
     barrier = pltpu.get_barrier_semaphore()
     for at in AROUND:
-        @pl.when(jnp.logical_not(awaited(at[0])))
+        @pl.when(jnp.logical_not(awaited(*at)))
         def _():
             pl.semaphore_signal(barrier, inc=1, device_id=device(*at), device_id_type=MESH)
 
@@ -153,13 +156,10 @@
         send_cols[0, g] = head
         send_cols[1, g] = tail
 
-    def exchange():
-        n = len(AROUND) - jnp.where(ex == 0, 3, 0)
-        pl.semaphore_wait(barrier, n)
-        for (dx, dy), copy in zip(AROUND, copies):
-            pl.when(jnp.logical_not(answers(dx)))(copy.start)
-
-    pl.when(jnp.logical_not(cloud_first))(exchange)
+    n_mutual = sum(jnp.where(answers(*at), 0, 1) for at in AROUND)
+    pl.semaphore_wait(barrier, n_mutual)
+    for at, copy in zip(AROUND, copies):
+        pl.when(jnp.logical_not(answers(*at)))(copy.start)
 
     small[1].wait()
     small[2].wait()
@@ -238,8 +238,6 @@
         part = pl.ds(c * per, per)
         outs.append(pltpu.make_async_copy(crm_new.at[part], crm_hbm_out.at[part], out_sem.at[c]))
         outs[-1].start()
-
-    pl.when(cloud_first)(exchange)
 
     def spread(c, e):
         lane = lax.broadcasted_iota(jnp.int32, c.shape, 1)
@@ -269,17 +267,32 @@
         change = [part for j in range(SETS) for part in split(temp[1, j, padded, :])]
         result[here, :] += dot(change, mean[...])
 
-    def take(dx):
-        for k, at in enumerate(AROUND):
-            if at[0] == dx:
-                copies[k].wait_recv()
+    def take(k):
+        copies[k].wait_recv()
+        back = AROUND.index((-AROUND[k][0], -AROUND[k][1]))
+        pl.when(answers(*AROUND[back]))(copies[back].start)
+
+    def add_rows(end, h1, h2, h3, e1, e2):
+        u, v = spread(h1, e1)
+        w, _ = spread(u + h2, v + e2)
+        for r, add in enumerate((3.0 * (w + h1) + h3, 3.0 * u + h2, h1)):
+            result[pl.ds(CX - 1 - r if end else r, GLEV, stride=CX), :] += 0.008 * add
+
+    nothing = jnp.zeros((GLEV, CY), F32)
+    for dx in (-1, 1):
+        take(AROUND.index((dx, 0)))
+        end = (1 - dx) // 2
+        add_rows(end, *(recv_rows[end, r] for r in range(HALO)), nothing, nothing)
 
     low_lanes = lane8 % 8 < 4
     for side in range(2):
         edge[side, 0:8, :] = zero
         edge[side, 16:24, :] = zero
 
-    take(0)
+    for dy in (-1, 1):
+        for k, at in enumerate(AROUND):
+            if at[1] == dy:
+                take(k)
     for g in range(PACKS):
         sides = []
         for side in range(2):
@@ -305,21 +318,12 @@
         own = pl.ds(levels[0] * CX, len(levels) * CX)
         result[own, :] += jnp.where((lane < 3) | (lane >= CY - 3), add, 0.0)
 
-    for dx in (-1, 1):
-        take(dx)
-        end = (1 - dx) // 2
+    for end in range(2):
         far = [jnp.where(low_lanes, recv_far[end, 1, r], recv_far[end, 0, r]) for r in range(2)]
         e1, e2 = (
             jnp.concatenate([pltpu.roll(x, 128 - 8 * g, 1) if g else x for g in range(GROUPS)]) for x in far
         )
-        h1, h2, h3 = (recv_rows[end, r] for r in range(HALO))
-        u, v = spread(h1, e1)
-        w, _ = spread(u + h2, v + e2)
-        for r, add in enumerate((3.0 * (w + h1) + h3, 3.0 * u + h2, h1)):
-            result[pl.ds(CX - 1 - r if end else r, GLEV, stride=CX), :] += 0.008 * add
-        for (ax, _), copy in zip(AROUND, copies):
-            if ax == -dx:
-                pl.when(answers(ax))(copy.start)
+        add_rows(end, nothing, nothing, nothing, e1, e2)
     outs.append(pltpu.make_async_copy(result, dyn_hbm_out, out_sem.at[CHUNKS]))
     outs[-1].start()
     for copy in copies:

time: 35.5 us -> 28.3 us (0.80)
  the two profiles are of different devices: /device:TPU:126 before, /device:TPU:2 now
where the time goes in v5:
time: 28.3 us; the launch traced here: 28.1 us
  Pallas kernels  27.4 us (97%)
  between operations  0.64 us (2%)
    pallas_call x1, Pallas kernels, shards(): pl.pallas_call(functools.partial(kernel, sizes), out_shape=(dyn_shape, cr...  25.4 us
    pallas_call x1, Pallas kernels, shards(): pl.pallas_call(write, out_shape=(dyn_shape, crm_shape), in_specs=[hbm] *...  2.08 us

profile of v5, /device:TPU:2, one launch (start us, length us, event | category | flops | bytes accessed | tf_op | source)
XLA Modules:
  0.0 28.1 jit_solution(10467274309748747155)
XLA Ops:
  0.6 25.4 %shard_map.59 = (f32[576,128]{1,0:T(8,128)}, f32[1856,128]{1,0:T(8,128)}) custom-call(s32[1,32]{1,0:T(1,128)} %bitcast.12, s32[1,32]{1,0:T(1,128)} %bitcast.13, f32[576,128]{1,0:T(8,128)} %bitcast.11, f32[1856,128]{1,0:T(8,128)} %bitcast.10), custom_call_target="tpu_custom_call" | custom-call | tf_op jit(solution)/shard_map/pallas_call | solution.py:357
  26.0 2.1 %shard_map.60 = (f32[576,128]{1,0:T(8,128)}, f32[1856,128]{1,0:T(8,128)}) custom-call(f32[576,128]{1,0:T(8,128)} %get-tuple-element.6.result, f32[1856,128]{1,0:T(8,128)} %get-tuple-element.7.crm_new), custom_call_target="tpu_custom_call" | custom-call | tf_op jit(solution)/shard_map/pallas_call | solution.py:398

commit v6 on v5

--- a/solution.py
+++ b/solution.py
@@ -69,7 +69,7 @@
     dyn_hbm_out, crm_hbm_out,
     result, crm_new, field, crm, sub, slot, step, pick, mean, temp, moist, pull,
     tall, send_rows, recv_rows, send_cols, recv_cols, send_far, recv_far, edge,
-    load_sem, in_sem, out_sem, send_sem, recv_sem,
+    load_sem, in_sem, out_sem, send_sem, recv_sem, ready_sem,
 ):
     nex, ney = sizes
     ex, ey = lax.axis_index("ex"), lax.axis_index("ey")
@@ -83,14 +83,19 @@
     def answers(dx, dy):
         x, y = device(dx, dy)
         to_first = (x == 0) & (y == 0) & jnp.logical_not(last_ey)
-        return to_first | (ey == 0) if dy == -1 else to_first
+        return to_first | (ey == 0) | last_ey if dy == -1 else to_first
 
     def awaited(dx, dy):
-        return last_ey | first if dy == 1 else first if dy == 0 else first & (ey > 0)
+        if dy == 1:
+            return last_ey | first | (ey == ney - 2)
+        return first if dy == 0 else first & (ey > 0)
+
+    def indirect(dx, dy):
+        return last_ey if dy == 0 else ey < 0
 
     barrier = pltpu.get_barrier_semaphore()
     for at in AROUND:
-        @pl.when(jnp.logical_not(awaited(*at)))
+        @pl.when(jnp.logical_not(awaited(*at) | indirect(*at)))
         def _():
             pl.semaphore_signal(barrier, inc=1, device_id=device(*at), device_id_type=MESH)
 
@@ -156,10 +161,14 @@
         send_cols[0, g] = head
         send_cols[1, g] = tail
 
-    n_mutual = sum(jnp.where(answers(*at), 0, 1) for at in AROUND)
-    pl.semaphore_wait(barrier, n_mutual)
+    n_answers = sum(jnp.where(answers(*at), 1, 0) for at in AROUND)
+    pl.semaphore_wait(barrier, len(AROUND) - n_answers - jnp.where(last_ey, 2, 0))
+    for at in AROUND:
+        @pl.when(awaited(*at))
+        def _():
+            pl.semaphore_signal(ready_sem, inc=1, device_id=device(*at), device_id_type=MESH)
     for at, copy in zip(AROUND, copies):
-        pl.when(jnp.logical_not(answers(*at)))(copy.start)
+        pl.when(jnp.logical_not(answers(*at) | indirect(*at)))(copy.start)
 
     small[1].wait()
     small[2].wait()
@@ -268,9 +277,10 @@
         result[here, :] += dot(change, mean[...])
 
     def take(k):
-        copies[k].wait_recv()
-        back = AROUND.index((-AROUND[k][0], -AROUND[k][1]))
-        pl.when(answers(*AROUND[back]))(copies[back].start)
+        if k == from_across:
+            pl.when(jnp.logical_not(last_ey))(copies[k].wait_recv)
+        else:
+            copies[k].wait_recv()
 
     def add_rows(end, h1, h2, h3, e1, e2):
         u, v = spread(h1, e1)
@@ -278,52 +288,73 @@
         for r, add in enumerate((3.0 * (w + h1) + h3, 3.0 * u + h2, h1)):
             result[pl.ds(CX - 1 - r if end else r, GLEV, stride=CX), :] += 0.008 * add
 
+    @pl.when(n_answers > 0)
+    def _():
+        pl.semaphore_wait(ready_sem, n_answers)
+
+    for at, copy in zip(AROUND, copies):
+        pl.when(answers(*at))(copy.start)
+    from_across = AROUND.index((0, -1))
+
+    @pl.when(last_ey)
+    def _():
+        copies[from_across].wait_recv()
+        for at, copy in zip(AROUND, copies):
+            if at[1] == 0:
+                copy.start()
+
     nothing = jnp.zeros((GLEV, CY), F32)
     for dx in (-1, 1):
         take(AROUND.index((dx, 0)))
         end = (1 - dx) // 2
         add_rows(end, *(recv_rows[end, r] for r in range(HALO)), nothing, nothing)
 
-    low_lanes = lane8 % 8 < 4
-    for side in range(2):
-        edge[side, 0:8, :] = zero
-        edge[side, 16:24, :] = zero
+    tiles = 2 * PACKS
+    for i in range(tiles):
+        edge[24 * i : 24 * i + 8, :] = zero
+        edge[24 * i + 16 : 24 * i + 24, :] = zero
+    slot8 = lane8 % 8
+    low_lanes = slot8 < 4
 
     for dy in (-1, 1):
         for k, at in enumerate(AROUND):
             if at[1] == dy:
                 take(k)
+    for i in range(tiles):
+        side, g = i // PACKS, i % PACKS
+        beyond = (slot8 >= 5) if side == 0 else (slot8 < 3)
+        edge[24 * i + 8 : 24 * i + 16, :] = jnp.where(beyond, recv_cols[side, g], 0.0)
+    at = [
+        jnp.concatenate([edge[pl.ds(24 * i + 8 + k, 8), :] for i in range(tiles)]) for k in range(-HALO, HALO + 1)
+    ]
+    c0, c1, c2, c3 = at[3], at[2] + at[4], at[1] + at[5], at[0] + at[6]
+    slots = lax.broadcasted_iota(jnp.int32, c0.shape, 1) % 8
+    valid = (slots >= 5) | (slots < 3)
+
+    def near(x):
+        return x + jnp.where(valid, pltpu.roll(x, 1, 1) + pltpu.roll(x, CY - 1, 1), 0.0)
+
+    far = [jnp.where(low_lanes, recv_far[end, 1, r], recv_far[end, 0, r]) for r in range(2) for end in range(2)]
+    far = [
+        jnp.concatenate([pltpu.roll(x, 128 - 8 * g, 1) if g else x for x in far[2 * r : 2 * r + 2] for g in range(GROUPS)])
+        for r in range(2)
+    ]
+    u, v = spread(jnp.zeros_like(far[0]), far[0])
+    x = near(c0)
+    w, _ = spread(u, v + far[1])
+    x = near(x + 3.0 * c1)
+    x = 0.008 * near(x + (6.0 * c0 + 3.0 * c2))
+    for end in range(2):
+        part = slice(end * GLEV, end * GLEV + GLEV)
+        for r, add in enumerate((3.0 * w[part], 3.0 * u[part])):
+            result[pl.ds(CX - 1 - r if end else r, GLEV, stride=CX), :] += 0.008 * add
     for g in range(PACKS):
-        sides = []
-        for side in range(2):
-            halo = recv_cols[side, g]
-            beyond = (lane8 % 8 >= 5) if side == 0 else (lane8 % 8 < 3)
-            valid = (lane8 % 8 >= 5) | (lane8 % 8 < 3)
-            halo = jnp.where(beyond, halo, 0.0)
-            edge[side, 8:16, :] = halo
-            at = [edge[side, 8 + k : 16 + k, :] for k in range(-HALO, HALO + 1)]
-            c0, c1, c2, c3 = halo, at[2] + at[4], at[1] + at[5], at[0] + at[6]
-
-            def near(x):
-                return x + jnp.where(valid, pltpu.roll(x, 1, 1) + pltpu.roll(x, CY - 1, 1), 0.0)
-
-            x = near(c0)
-            x = near(x + 3.0 * c1)
-            x = near(x + (6.0 * c0 + 3.0 * c2))
-            sides.append(0.008 * x)
-        both = jnp.where(low_lanes, sides[0], sides[1])
+        both = jnp.where(low_lanes, x[8 * g : 8 * g + 8], x[8 * (g + PACKS) : 8 * (g + PACKS) + 8])
         levels = range(g * PACK, min(GLEV, g * PACK + PACK))
-        add = jnp.concatenate([pltpu.roll(both, (128 - 8 * (i % PACK)) % 128, 1) if i % PACK else both for i in levels])
+        add = jnp.concatenate([pltpu.roll(both, 128 - 8 * (i % PACK), 1) if i % PACK else both for i in levels])
         lane = lax.broadcasted_iota(jnp.int32, add.shape, 1)
         own = pl.ds(levels[0] * CX, len(levels) * CX)
         result[own, :] += jnp.where((lane < 3) | (lane >= CY - 3), add, 0.0)
-
-    for end in range(2):
-        far = [jnp.where(low_lanes, recv_far[end, 1, r], recv_far[end, 0, r]) for r in range(2)]
-        e1, e2 = (
-            jnp.concatenate([pltpu.roll(x, 128 - 8 * g, 1) if g else x for g in range(GROUPS)]) for x in far
-        )
-        add_rows(end, nothing, nothing, nothing, e1, e2)
     outs.append(pltpu.make_async_copy(result, dyn_hbm_out, out_sem.at[CHUNKS]))
     outs[-1].start()
     for copy in copies:
@@ -379,12 +410,13 @@
             pltpu.VMEM((2, PACKS, 8, 128), F32),
             pltpu.VMEM((2, 2, 2, 8, 128), F32),
             pltpu.VMEM((2, 2, 2, 8, 128), F32),
-            pltpu.VMEM((2, 24, 128), F32),
+            pltpu.VMEM((2 * PACKS * 24, 128), F32),
             pltpu.SemaphoreType.DMA((3,)),
             pltpu.SemaphoreType.DMA((CHUNKS,)),
             pltpu.SemaphoreType.DMA((CHUNKS + 1,)),
             pltpu.SemaphoreType.DMA((8,)),
             pltpu.SemaphoreType.DMA((8,)),
+            pltpu.SemaphoreType.REGULAR,
         ],
         compiler_params=pltpu.CompilerParams(
             collective_id=0, has_side_effects=True, vmem_limit_bytes=VMEM_BYTES

time: 28.3 us -> 25.5 us (0.901)
  the two profiles are of different devices: /device:TPU:2 before, /device:TPU:96 now
where the time goes in v6:
time: 25.5 us; the launch traced here: 25.3 us
  Pallas kernels  24.7 us (97%)
  between operations  0.64 us (3%)
    pallas_call x1, Pallas kernels, shards(): pl.pallas_call(functools.partial(kernel, sizes), out_shape=(dyn_shape, cr...  22.6 us
    pallas_call x1, Pallas kernels, shards(): pl.pallas_call(write, out_shape=(dyn_shape, crm_shape), in_specs=[hbm] *...  2.08 us

profile of v6, /device:TPU:96, one launch (start us, length us, event | category | flops | bytes accessed | tf_op | source)
XLA Modules:
  0.0 25.3 jit_solution(7918173124620966669)
XLA Ops:
  0.6 22.6 %shard_map.59 = (f32[576,128]{1,0:T(8,128)}, f32[1856,128]{1,0:T(8,128)}) custom-call(s32[1,32]{1,0:T(1,128)} %bitcast.12, s32[1,32]{1,0:T(1,128)} %bitcast.13, f32[576,128]{1,0:T(8,128)} %bitcast.11, f32[1856,128]{1,0:T(8,128)} %bitcast.10), custom_call_target="tpu_custom_call" | custom-call | tf_op jit(solution)/shard_map/pallas_call | solution.py:388
  23.2 2.1 %shard_map.60 = (f32[576,128]{1,0:T(8,128)}, f32[1856,128]{1,0:T(8,128)}) custom-call(f32[576,128]{1,0:T(8,128)} %get-tuple-element.6.result, f32[1856,128]{1,0:T(8,128)} %get-tuple-element.7.crm_new), custom_call_target="tpu_custom_call" | custom-call | tf_op jit(solution)/shard_map/pallas_call | solution.py:430

commit v7 on v6

--- a/solution.py
+++ b/solution.py
@@ -355,8 +355,8 @@
         lane = lax.broadcasted_iota(jnp.int32, add.shape, 1)
         own = pl.ds(levels[0] * CX, len(levels) * CX)
         result[own, :] += jnp.where((lane < 3) | (lane >= CY - 3), add, 0.0)
-    outs.append(pltpu.make_async_copy(result, dyn_hbm_out, out_sem.at[CHUNKS]))
-    outs[-1].start()
+        outs.append(pltpu.make_async_copy(result.at[own], dyn_hbm_out.at[own], out_sem.at[CHUNKS + g]))
+        outs[-1].start()
     for copy in copies:
         copy.wait_send()
     for out in outs:
@@ -413,7 +413,7 @@
             pltpu.VMEM((2 * PACKS * 24, 128), F32),
             pltpu.SemaphoreType.DMA((3,)),
             pltpu.SemaphoreType.DMA((CHUNKS,)),
-            pltpu.SemaphoreType.DMA((CHUNKS + 1,)),
+            pltpu.SemaphoreType.DMA((CHUNKS + PACKS,)),
             pltpu.SemaphoreType.DMA((8,)),
             pltpu.SemaphoreType.DMA((8,)),
             pltpu.SemaphoreType.REGULAR,

time: 25.5 us -> 25.5 us (level)
  no operation moved by 1% of the time
where the time goes in v7:
time: 25.5 us; the launch traced here: 25.3 us
  Pallas kernels  24.7 us (97%)
  between operations  0.64 us (3%)
    pallas_call x1, Pallas kernels, shards(): pl.pallas_call(functools.partial(kernel, sizes), out_shape=(dyn_shape, cr...  22.6 us
    pallas_call x1, Pallas kernels, shards(): pl.pallas_call(write, out_shape=(dyn_shape, crm_shape), in_specs=[hbm] *...  2.08 us

profile of v7, /device:TPU:96, one launch (start us, length us, event | category | flops | bytes accessed | tf_op | source)
XLA Modules:
  0.0 25.3 jit_solution(18307400677601812851)
XLA Ops:
  0.6 22.6 %shard_map.59 = (f32[576,128]{1,0:T(8,128)}, f32[1856,128]{1,0:T(8,128)}) custom-call(s32[1,32]{1,0:T(1,128)} %bitcast.12, s32[1,32]{1,0:T(1,128)} %bitcast.13, f32[576,128]{1,0:T(8,128)} %bitcast.11, f32[1856,128]{1,0:T(8,128)} %bitcast.10), custom_call_target="tpu_custom_call" | custom-call | tf_op jit(solution)/shard_map/pallas_call | solution.py:388
  23.2 2.1 %shard_map.60 = (f32[576,128]{1,0:T(8,128)}, f32[1856,128]{1,0:T(8,128)}) custom-call(f32[576,128]{1,0:T(8,128)} %get-tuple-element.6.result, f32[1856,128]{1,0:T(8,128)} %get-tuple-element.7.crm_new), custom_call_target="tpu_custom_call" | custom-call | tf_op jit(solution)/shard_map/pallas_call | solution.py:430
